TPU v7x, 256 devices: a whole 4x4x8 slice. The times are simulated.
256 devices in a mesh: dp: 16 (over y_hi, x, core), fsdp: 16 (over z, y_lo).
Axes of the slice: x: 4, y: 4 (y_hi: 2, y_lo: 2; y = y_hi * 2 + y_lo), z: 8, core: 2. Of those that a mesh axis runs over, the one named last changes fastest.
Arguments:
- cotangent: bfloat16 [32768, 2560], P(('dp', 'fsdp')), may hold values from -6 to 6
- out_weight: bfloat16 [1280, 2560], P('fsdp'), may hold values from -0.15625 to 0.15625
- queries: bfloat16 [49152, 1280], P(('dp', 'fsdp')), may hold values from -200 to 200
- key_vectors: bfloat16 [49152, 1280], P(('dp', 'fsdp')), may hold values from -5 to 5
- value_vectors: bfloat16 [49152, 1280], P(('dp', 'fsdp')), may hold values from -6 to 6
- destination: int32 [32768], P(('dp', 'fsdp')), may hold values from 0 to 3071, as said below
- protein_ids: int32 [49152], P(('dp', 'fsdp')), may hold values from -192 to 79, as said below
Outputs:
- query_grad: bfloat16 [49152, 1280], P(('dp', 'fsdp'))
- key_grad: bfloat16 [49152, 1280], P(('dp', 'fsdp'))
- value_grad: bfloat16 [49152, 1280], P(('dp', 'fsdp'))
- weight_grad: float32 [1280, 2560], P('fsdp')
Inputs may be any that keep to these rules, and one draw needn't show every extreme that they name: `destination`: in each fsdp group every owner uses a prefix of its 192 slots and each used slot is named by exactly one token row of the group; at most 12 rows of one device go to one owner, and in every group the last owner uses all 192 slots and receives exactly 12 rows from every device. `protein_ids`: used slots of owner o hold ids 5 * o to 5 * o + 4, in contiguous runs; unused slot s of an owner holds -1 - s; in every group the last owner holds 5 proteins.
All inputs are finite; a program needn't handle non-finite values.
Results may differ from a plain program's by a relative error of at most 0.0058.
Values may be sent and summed in bfloat16 or wider, within the bound.
A program may use at most 128 MiB of HBM per device.

v0:
```python
import math

import jax
import jax.numpy as jnp
from jax import lax
from jax.sharding import PartitionSpec as P

HEADS = 20
HEAD = 64


def heads_of(matrix, col_begin):
    return matrix[:, col_begin : col_begin + 5 * HEAD].reshape(matrix.shape[0], 5, HEAD)


def owner_backward(query_rows, key_rows, value_rows, grad_rows, slot_ids):
    row_count = query_rows.shape[0]
    same_protein = slot_ids[:, None] == slot_ids[None, :]
    live_rows = (slot_ids >= 0)[:, None]
    score_scale = 1.0 / math.sqrt(HEAD)
    query_parts, key_parts, value_parts, attended_parts = ([], [], [], [])
    for head_first in range(0, HEADS, 5):
        col_begin = head_first * HEAD
        query_part = heads_of(query_rows, col_begin)
        key_part = heads_of(key_rows, col_begin)
        value_part = heads_of(value_rows, col_begin)
        grad_part = heads_of(grad_rows, col_begin)
        scores = (
            jnp.einsum("qhd,khd->hqk", query_part, key_part, preferred_element_type=jnp.float32)
            * score_scale
        )
        scores = jnp.where(same_protein[None], scores, -1e30)
        row_max = jnp.max(scores, axis=2, keepdims=True)
        exponent = jnp.exp(scores - row_max)
        softmax = exponent / jnp.sum(exponent, axis=2, keepdims=True)
        rounded = softmax.astype(jnp.bfloat16)
        attended = jnp.einsum(
            "hqk,khd->qhd", rounded, value_part, preferred_element_type=jnp.float32
        )
        value_grad = jnp.einsum(
            "hqk,qhd->khd", rounded, grad_part, preferred_element_type=jnp.float32
        )
        prob_grad = jnp.einsum(
            "qhd,khd->hqk", grad_part, value_part, preferred_element_type=jnp.float32
        )
        delta = jnp.sum(softmax * prob_grad, axis=2, keepdims=True)
        score_grad = (softmax * (prob_grad - delta)).astype(jnp.bfloat16)
        query_grad = (
            jnp.einsum("hqk,khd->qhd", score_grad, key_part, preferred_element_type=jnp.float32)
            * score_scale
        )
        key_grad = (
            jnp.einsum("hqk,qhd->khd", score_grad, query_part, preferred_element_type=jnp.float32)
            * score_scale
        )
        query_parts.append(query_grad.reshape(row_count, 5 * HEAD))
        key_parts.append(key_grad.reshape(row_count, 5 * HEAD))
        value_parts.append(value_grad.reshape(row_count, 5 * HEAD))
        attended_parts.append(attended.reshape(row_count, 5 * HEAD))
    query_all = jnp.where(live_rows, jnp.concatenate(query_parts, axis=1), 0.0).astype(jnp.bfloat16)
    key_all = jnp.where(live_rows, jnp.concatenate(key_parts, axis=1), 0.0).astype(jnp.bfloat16)
    value_all = jnp.where(live_rows, jnp.concatenate(value_parts, axis=1), 0.0).astype(jnp.bfloat16)
    attended_all = jnp.concatenate(attended_parts, axis=1).astype(jnp.bfloat16)
    return (query_all, key_all, value_all, attended_all)


def per_device(
    cotangent, out_weight, queries, key_vectors, value_vectors, destination, protein_ids
):
    own_rows = queries.shape[0]
    width = queries.shape[1]
    groups = lax.axis_size("fsdp")
    per_pair = own_rows // groups
    owner_of = destination // own_rows
    slot_of = destination % own_rows
    earlier = (owner_of[None, :] == owner_of[:, None]) & (slot_of[None, :] < slot_of[:, None])
    position = owner_of * per_pair + jnp.sum(earlier, axis=1)
    send_slots = jnp.full((groups * per_pair,), own_rows, jnp.int32).at[position].set(slot_of)
    out_grad = jnp.einsum(
        "nd,hd->nh",
        cotangent,
        lax.all_gather(out_weight, "fsdp", axis=0, tiled=True),
        preferred_element_type=jnp.float32,
    ).astype(jnp.bfloat16)
    outgoing = jnp.zeros((groups * per_pair, width), jnp.bfloat16).at[position].set(out_grad)
    incoming, incoming_slots = (
        lax.all_to_all(outgoing, "fsdp", split_axis=0, concat_axis=0, tiled=True),
        lax.all_to_all(send_slots, "fsdp", split_axis=0, concat_axis=0, tiled=True),
    )
    slot_grad = (
        jnp.zeros((own_rows, width), jnp.bfloat16).at[incoming_slots].set(incoming, mode="drop")
    )
    query_grad, key_grad, value_grad, attended_all = owner_backward(
        queries, key_vectors, value_vectors, slot_grad, protein_ids
    )
    returning = attended_all[jnp.minimum(incoming_slots, own_rows - 1)]
    returned = lax.all_to_all(returning, "fsdp", split_axis=0, concat_axis=0, tiled=True)
    token_out = returned[position]
    part_rows = lax.slice_in_dim(token_out, 0, out_weight.shape[0] * lax.axis_size("fsdp"), axis=1)
    local_sum = lax.psum_scatter(
        jnp.einsum("nh,nd->hd", part_rows, cotangent, preferred_element_type=jnp.float32),
        "fsdp",
        scatter_dimension=0,
        tiled=True,
    )
    weight_grad = lax.psum(local_sum, "dp")
    return (query_grad, key_grad, value_grad, weight_grad)


def solution(mesh):
    return jax.shard_map(
        per_device,
        mesh=mesh,
        in_specs=(
            P(("dp", "fsdp"), None),
            P("fsdp", None),
            P(("dp", "fsdp"), None),
            P(("dp", "fsdp"), None),
            P(("dp", "fsdp"), None),
            P(("dp", "fsdp")),
            P(("dp", "fsdp")),
        ),
        out_specs=(
            P(("dp", "fsdp"), None),
            P(("dp", "fsdp"), None),
            P(("dp", "fsdp"), None),
            P("fsdp", None),
        ),
        check_vma=False,
    )
```

profile of v0, /device:TPU:1, one launch (start us, length us, event | category | flops | bytes accessed | tf_op | source)
XLA Modules:
  0.0 608.2 jit_solution(10199907372836193788)
XLA Ops:
  7.2 0.7 all-gather.2.cloned.1.call-update
  7.9 0.7 and_select_fusion.1
  8.8 1.0 scatter_custom_fusion
  9.8 0.7 all_to_all.24
  10.5 10.1 %all-to-all-start = ((s32[16,12,1]{1,2,0:T(1,128)}), s32[16,12,1]{1,2,0:T(1,128)S(1)}, u32[]{:S(2)}, u32[]{:S(2)}) async-start(s32[16,12,1]{1,2,0:T(1,128)} %bitcast.2), calls=%async_computation | async-start | bytes 16384 | tf_op jit(solution)/shard_map/all_to_all | solution.py:88
  20.6 1.3 fusion.46
  22.5 1.4 fusion.49
  24.4 1.5 fusion.47
  26.5 1.5 fusion.52
  28.7 1.5 fusion.50
  30.9 1.5 fusion.51
  35.7 0.7 reduce.3
  36.5 1.1 gather_fusion
  37.5 0.9 all_to_all.30
  38.5 7.5 %all-to-all-start.2 = ((bf16[16,12,1280]{2,1,0:T(8,128)(2,1)}), bf16[16,12,1280]{2,1,0:T(8,128)(2,1)S(1)}, u32[]{:S(2)}, u32[]{:S(2)}) async-start(bf16[16,12,1280]{2,1,0:T(8,128)(2,1)} %all_to_all.30), calls=%async_computation.2 | async-start | bytes 1310720 | tf_op jit(solution)/shard_map/all_to_all | solution.py:97
  46.2 0.7 pad_clamp_fusion
  46.9 24.7 %all-to-all-done.2 = bf16[16,12,1280]{2,1,0:T(8,128)(2,1)S(1)} async-done(((bf16[16,12,1280]{2,1,0:T(8,128)(2,1)}), bf16[16,12,1280]{2,1,0:T(8,128)(2,1)S(1)}, u32[]{:S(2)}, u32[]{:S(2)}) %all-to-all-start.2) | async-done | bytes 491552 | tf_op jit(solution)/shard_map/all_to_all | solution.py:97
  71.7 0.9 gather_fusion.1
  72.6 6.5 %fusion.54 = f32[1280,2560]{1,0:T(8,128)} fusion(bf16[128,1280]{1,0:T(8,128)(2,1)S(1)} %gather_fusion.1, bf16[128,2560]{1,0:T(8,128)(2,1)S(1)} %copy-done), kind=kOutput, calls=%fused_computation.101 | convolution fusion | flops 838860800 | bytes 14090240 | tf_op jit(solution)/shard_map/nh,nd->hd/dot_general | solution.py:101
  79.2 86.9 %all-gather.2.cloned.1.call-done = bf16[1280,2560]{1,0:T(8,128)(2,1)} async-done(((bf16[80,2560]{1,0:T(8,128)(2,1)}), bf16[1280,2560]{1,0:T(8,128)(2,1)}) %all-gather.2.cloned.1.call-update) | async-done | bytes 6553616 | tf_op jit(solution)/shard_map/all_gather | solution.py:82
  166.1 5.8 convolution_convert_fusion
  171.9 1.8 scatter_custom_fusion.1
  173.7 0.9 all_to_all.27
  174.7 7.6 %all-to-all-start.1 = ((bf16[16,12,1280]{2,1,0:T(8,128)(2,1)}), bf16[16,12,1280]{2,1,0:T(8,128)(2,1)S(1)}, u32[]{:S(2)}, u32[]{:S(2)}) async-start(bf16[16,12,1280]{2,1,0:T(8,128)(2,1)} %all_to_all.27), calls=%async_computation.1 | async-start | bytes 1310720 | tf_op jit(solution)/shard_map/all_to_all | solution.py:87
  182.3 25.5 %all-to-all-done.1 = bf16[16,12,1280]{2,1,0:T(8,128)(2,1)S(1)} async-done(((bf16[16,12,1280]{2,1,0:T(8,128)(2,1)}), bf16[16,12,1280]{2,1,0:T(8,128)(2,1)S(1)}, u32[]{:S(2)}, u32[]{:S(2)}) %all-to-all-start.1) | async-done | bytes 491552 | tf_op jit(solution)/shard_map/all_to_all | solution.py:87
  207.8 0.9 reshape.273
  208.7 2.3 scatter_custom_fusion.2
  211.0 0.9 fusion.48
  211.9 1.7 copy.170
  213.6 1.0 copy.165
  214.6 1.8 copy.160
  216.5 2.3 fusion.20
  218.8 2.1 fusion.26
  221.0 2.3 fusion.23
  223.3 1.8 multiply_reduce_fusion.1
  225.1 1.5 multiply_convert_fusion.1
  226.6 1.9 convolution_multiply_fusion.9
  228.5 0.9 convolution_multiply_fusion.5
  232.2 222.3 %reduce-scatter.2.cloned.1.call-done = f32[80,2560]{1,0:T(8,128)} async-done(((f32[1280,2560]{1,0:T(8,128)}), f32[80,2560]{1,0:T(8,128)}) %reduce-scatter.2.cloned.1.call-update) | async-done | bytes 819216 | tf_op jit(solution)/shard_map/reduce_scatter | solution.py:100
  454.5 2.2 fusion.17
  456.8 1.1 copy.191
  458.1 1.1 copy.189
  459.5 1.7 copy.190
  461.5 1.1 copy.192
  463.1 1.2 concatenate.15
  465.2 1.3 select_convert_fusion
  466.5 133.0 %all-reduce.2.cloned.1.call-done = f32[80,2560]{1,0:T(8,128)} async-done(((f32[80,2560]{1,0:T(8,128)}), f32[80,2560]{1,0:T(8,128)}) %all-reduce.2.cloned.1.call-update) | async-done | bytes 819216 | tf_op jit(solution)/shard_map/psum | solution.py:106
  599.5 2.1 copy.218
  (132 shorter events, 12.1 us)
Async XLA Ops:
  7.2 65.4 %copy-start = (bf16[128,2560]{1,0:T(8,128)(2,1)S(1)}, bf16[128,2560]{1,0:T(8,128)(2,1)}, u32[]{:S(2)}) copy-start(bf16[128,2560]{1,0:T(8,128)(2,1)} %param.7) | copy-start | bytes 1966084
  7.2 19.2 %copy-start.33 = (s32[192]{0:T(256)S(1)}, s32[192]{0:T(256)}, u32[]{:S(2)}) copy-start(s32[192]{0:T(256)} %param.13) | copy-start | bytes 2308
  7.2 158.9 %all-gather.2.cloned.1.call-start = ((), (), s32[]{:S(2)}) async-start(), calls=%async_computation.4 | async-start | bytes 6963200 | tf_op jit(solution)/shard_map/all_gather | solution.py:82
  8.8 13.1 %copy-start.35 = (s32[128]{0:T(128)}, s32[128]{0:T(128)S(1)}, u32[]{:S(2)}) copy-start(s32[128]{0:T(128)S(1)} %compare_select_fusion.2) | copy-start | bytes 1540
  10.5 24.7 %all-to-all-start = ((s32[16,12,1]{1,2,0:T(1,128)}), s32[16,12,1]{1,2,0:T(1,128)S(1)}, u32[]{:S(2)}, u32[]{:S(2)}) async-start(s32[16,12,1]{1,2,0:T(1,128)} %bitcast.2), calls=%async_computation | async-start | bytes 16384 | tf_op jit(solution)/shard_map/all_to_all | solution.py:88
  22.3 7.9 %copy-start.3 = (bf16[192,320]{0,1:T(8,128)(2,1)}, bf16[192,320]{0,1:T(8,128)(2,1)S(1)}, u32[]{:S(2)}) copy-start(bf16[192,320]{0,1:T(8,128)(2,1)S(1)} %copy.152) | copy-start | bytes 368644
  22.5 7.7 %copy-start.8 = (bf16[192,320]{0,1:T(8,128)(2,1)}, bf16[192,320]{0,1:T(8,128)(2,1)S(1)}, u32[]{:S(2)}) copy-start(bf16[192,320]{0,1:T(8,128)(2,1)S(1)} %copy.163) | copy-start | bytes 368644
  24.2 6.6 %copy-start.5 = (bf16[192,320]{0,1:T(8,128)(2,1)}, bf16[192,320]{0,1:T(8,128)(2,1)S(1)}, u32[]{:S(2)}) copy-start(bf16[192,320]{0,1:T(8,128)(2,1)S(1)} %copy.153) | copy-start | bytes 368644
  24.4 6.5 %copy-start.10 = (bf16[192,320]{0,1:T(8,128)(2,1)}, bf16[192,320]{0,1:T(8,128)(2,1)S(1)}, u32[]{:S(2)}) copy-start(bf16[192,320]{0,1:T(8,128)(2,1)S(1)} %copy.164) | copy-start | bytes 368644
  26.0 7.5 %copy-start.14 = (bf16[192,320]{0,1:T(8,128)(2,1)}, bf16[192,320]{0,1:T(8,128)(2,1)S(1)}, u32[]{:S(2)}) copy-start(bf16[192,320]{0,1:T(8,128)(2,1)S(1)} %copy.171) | copy-start | bytes 368644
  26.1 6.2 %copy-start.16 = (bf16[192,320]{0,1:T(8,128)(2,1)}, bf16[192,320]{0,1:T(8,128)(2,1)S(1)}, u32[]{:S(2)}) copy-start(bf16[192,320]{0,1:T(8,128)(2,1)S(1)} %copy.161) | copy-start | bytes 368644
  26.3 4.6 copy-start.18
  26.4 4.4 copy-start.20
  26.5 7.0 %copy-start.26 = (pred[192,192]{0,1:T(8,128)(4,1)}, pred[192,192]{0,1:T(8,128)(4,1)S(1)}, u32[]{:S(2)}) copy-start(pred[192,192]{0,1:T(8,128)(4,1)S(1)} %broadcast_compare_fusion) | copy-start | bytes 110596
  28.1 0.6 copy-start.31
  30.2 2.2 copy-start.29
  32.3 2.3 copy-start.27
  38.5 33.1 %all-to-all-start.2 = ((bf16[16,12,1280]{2,1,0:T(8,128)(2,1)}), bf16[16,12,1280]{2,1,0:T(8,128)(2,1)S(1)}, u32[]{:S(2)}, u32[]{:S(2)}) async-start(bf16[16,12,1280]{2,1,0:T(8,128)(2,1)} %all_to_all.30), calls=%async_computation.2 | async-start | bytes 1310720 | tf_op jit(solution)/shard_map/all_to_all | solution.py:97
  46.0 408.6 %reduce-scatter.2.cloned.1.call-start = ((), (), s32[]{:S(2)}) async-start(), calls=%async_computation.5 | async-start | bytes 13926400 | tf_op jit(solution)/shard_map/reduce_scatter | solution.py:100
  79.2 103.1 %copy-start.34 = (s32[192]{0:T(256)S(1)}, s32[192]{0:T(256)}, u32[]{:S(2)}) copy-start(s32[192]{0:T(256)} %param.13) | copy-start | bytes 2308
  79.2 137.3 %copy-start.9 = (bf16[192,320]{0,1:T(8,128)(2,1)S(1)}, bf16[192,320]{0,1:T(8,128)(2,1)}, u32[]{:S(2)}) copy-start(bf16[192,320]{0,1:T(8,128)(2,1)} %copy-done.8) | copy-start | bytes 368644
  79.2 137.3 %copy-start.32 = (f32[5,192]{1,0:T(8,128)S(1)}, f32[5,192]{1,0:T(8,128)}, u32[]{:S(2)}) copy-start(f32[5,192]{1,0:T(8,128)} %copy-done.31) | copy-start | bytes 11524
  171.9 47.0 %copy-start.4 = (bf16[192,320]{0,1:T(8,128)(2,1)S(1)}, bf16[192,320]{0,1:T(8,128)(2,1)}, u32[]{:S(2)}) copy-start(bf16[192,320]{0,1:T(8,128)(2,1)} %copy-done.3) | copy-start | bytes 368644
  171.9 47.0 %copy-start.6 = (bf16[192,320]{0,1:T(8,128)(2,1)S(1)}, bf16[192,320]{0,1:T(8,128)(2,1)}, u32[]{:S(2)}) copy-start(bf16[192,320]{0,1:T(8,128)(2,1)} %copy-done.5) | copy-start | bytes 368644
  171.9 47.0 %copy-start.30 = (f32[5,192]{1,0:T(8,128)S(1)}, f32[5,192]{1,0:T(8,128)}, u32[]{:S(2)}) copy-start(f32[5,192]{1,0:T(8,128)} %copy-done.29) | copy-start | bytes 11524
  174.7 33.2 %all-to-all-start.1 = ((bf16[16,12,1280]{2,1,0:T(8,128)(2,1)}), bf16[16,12,1280]{2,1,0:T(8,128)(2,1)S(1)}, u32[]{:S(2)}, u32[]{:S(2)}) async-start(bf16[16,12,1280]{2,1,0:T(8,128)(2,1)} %all_to_all.27), calls=%async_computation.1 | async-start | bytes 1310720 | tf_op jit(solution)/shard_map/all_to_all | solution.py:87
  182.2 417.3 %all-reduce.2.cloned.1.call-start = ((), (), s32[]{:S(2)}) async-start(), calls=%async_computation.6 | async-start | bytes 1638400 | tf_op jit(solution)/shard_map/psum | solution.py:106
  182.3 38.7 %copy-start.28 = (f32[5,192]{1,0:T(8,128)S(1)}, f32[5,192]{1,0:T(8,128)}, u32[]{:S(2)}) copy-start(f32[5,192]{1,0:T(8,128)} %copy-done.27) | copy-start | bytes 11524
  214.6 4.2 copy-start.25
  216.5 2.3 copy-start.23
  221.0 8.4 %copy-start.2 = (f32[5,192,192]{1,2,0:T(8,128)S(1)}, f32[5,192,192]{1,2,0:T(8,128)}, u32[]{:S(2)}) copy-start(f32[5,192,192]{1,2,0:T(8,128)} %get-tuple-element.28) | copy-start | bytes 2211844
  223.3 5.2 copy-start.11
  223.3 6.0 copy-start.19
  223.3 6.0 copy-start.24
  225.1 5.1 copy-start.7
  225.1 5.3 copy-start.1
  225.1 5.3 copy-start.17
  225.1 5.3 copy-start.22
  229.7 1.8 copy-start.15
  229.7 1.8 copy-start.21
  231.4 226.4 %copy-start.13 = (bf16[5,192,64]{1,2,0:T(8,128)(2,1)S(1)}, bf16[5,192,64]{1,2,0:T(8,128)(2,1)}, u32[]{:S(2)}) copy-start(bf16[5,192,64]{1,2,0:T(8,128)(2,1)} %convolution_multiply_fusion.5) | copy-start | bytes 368644
  231.5 226.5 %copy-start.12 = (bf16[5,192,64]{1,2,0:T(8,128)(2,1)S(1)}, bf16[5,192,64]{1,2,0:T(8,128)(2,1)}, u32[]{:S(2)}) copy-start(bf16[5,192,64]{1,2,0:T(8,128)(2,1)} %convolution_multiply_fusion.9) | copy-start | bytes 368644
Sparse Core Ops, SparseCore 0:
  9.8 156.2 all-gather.1
  168.7 285.7 reduce-scatter.1
  457.2 142.3 all-reduce.1
where the time goes:
time: 612 us; the launch traced here: 608 us
  waiting for transfers between devices  493 us (81%)
  matrix products  35.9 us (6%)
  local copies, waits for them, and re-layouts  33.5 us (5%)
  starting transfers between devices  25.5 us (4%)
  between operations  14.5 us (2%)
    reduce_scatter x1, waiting for transfers between devices, per_device(): lax.psum_scatter(jnp.einsum('nh,nd->hd', part_rows, cotangent, preferred_...  222 us
    psum x1, waiting for transfers between devices, per_device(): weight_grad = lax.psum(local_sum, 'dp')  133 us
    all_gather x1, waiting for transfers between devices, per_device(): lax.all_gather(out_weight, 'fsdp', axis=0, tiled=True)  86.9 us
    all_to_all x1, waiting for transfers between devices, per_device(): lax.all_to_all(outgoing, 'fsdp', split_axis=0, concat_axis=0, tiled=True)  25.5 us
    all_to_all x1, waiting for transfers between devices, per_device(): lax.all_to_all(returning, 'fsdp', split_axis=0, concat_axis=0, tiled=True)  24.7 us
  transfers between devices with their start and end apart: 6, of which 5 were waited for; matrix products, arithmetic and copies ran while one was open for 11% of the time, Pallas kernels for 0%

commit v1 on v0

v1 whole, which is shorter than its diff:
```python
import jax
import jax.numpy as jnp
from jax import lax
from jax.experimental import pallas as pl
from jax.experimental.pallas import tpu as pltpu
from jax.sharding import PartitionSpec as P

F32 = jnp.float32
BF16 = jnp.bfloat16
MESH = pl.DeviceIdType.MESH

NX, NY, NZ, NF = 4, 4, 8, 16
TOK = 128
OWN = 192
CAP = 12
D = 2560
QD = D // 4
ROWS = 80
PAIRS = 10
SCALE = 0.125


def fdiv(values, by):
    return jnp.floor((values + 0.5) * (1.0 / by))


def iota(shape, dim):
    return lax.broadcasted_iota(jnp.int32, shape, dim).astype(F32)


def dot_nt(a, b):
    return lax.dot_general(a, b, (((1,), (1,)), ((), ())), preferred_element_type=F32)


def dot_tn(a, b):
    return lax.dot_general(a, b, (((0,), (0,)), ((), ())), preferred_element_type=F32)


def dot_nn(a, b):
    return jnp.dot(a, b, preferred_element_type=F32)


def row_of(y, j):
    return 4 * (y // 2) + 2 * j + y % 2


def kernel(
    cot_hbm, w_hbm, q_hbm, k_hbm, v_hbm, dest_ref, ids_ref,
    dq_hbm, dk_hbm, dv_hbm, wg_hbm,
    cot_v, q_v, k_v, v_v, dq_v, dk_v, dv_v,
    dsend, drecv, packed, arrived, c_all,
    att, att_all, att_t, probs, same_v,
    w0, w1, g_tmp, g_v,
    s0, s1, r0, r1, t0, t1, u0, u1, vf, vb, zr, fall,
    load_sem, out_sem, wg_sem, own_sem,
    d_ssem, d_rsem, c_ssem, c_rsem,
    az_ssem, az_rsem, a1_ssem, a1_rsem, a2_ssem, a2_rsem,
    sib_ssem, sib_rsem,
    b2_ssem, b2_rsem, b1_ssem, b1_rsem, bz_ssem, bz_rsem,
    f1_ssem, f1_rsem, f2_ssem, f2_rsem, f3_ssem, f3_rsem,
):
    dp = lax.axis_index("dp")
    f = lax.axis_index("fsdp")
    c = dp % 2
    x = (dp // 2) % NX
    h = dp // 8
    z = f // 2
    y = 2 * h + f % 2

    def dev(x_, y_, z_, c_):
        return (((y_ // 2) * NX + x_) * 2 + c_, z_ * 2 + y_ % 2)

    def rcopy(src, dst, ssem, rsem, target):
        return pltpu.make_async_remote_copy(
            src_ref=src, dst_ref=dst, send_sem=ssem, recv_sem=rsem,
            device_id=target, device_id_type=MESH,
        )

    sibling = dev(x, y, z, 1 - c)

    loads = [
        pltpu.make_async_copy(src, dst, load_sem.at[i])
        for i, (src, dst) in enumerate(
            ((cot_hbm, cot_v), (q_hbm, q_v), (k_hbm, k_v), (v_hbm, v_v))
        )
    ]
    for load in loads:
        load.start()

    barrier = pltpu.get_barrier_semaphore()

    @pl.loop(1, NF)
    def _(s):
        pl.semaphore_signal(
            barrier, inc=1, device_id=(dp, (f + s) % NF), device_id_type=MESH
        )

    for s in range(1, 4):
        pl.semaphore_signal(
            barrier, inc=1, device_id=dev((x + s) % NX, y, z, c), device_id_type=MESH
        )
        pl.semaphore_signal(
            barrier, inc=1, device_id=dev(x, (y + s) % NY, z, c), device_id_type=MESH
        )
    pl.semaphore_signal(barrier, inc=1, device_id=sibling, device_id_type=MESH)
    pl.semaphore_wait(barrier, 22)

    active = z // 4 == c
    root = jnp.logical_and(active, (z % 4) // 2 == h)
    w_mine = w_hbm.at[:, pl.ds(pl.multiple_of(x * QD, 128), QD)]

    def spread_z(dst):
        pltpu.make_async_copy(w_mine, dst, own_sem).start()

        @pl.loop(1, NZ)
        def _(s):
            rcopy(
                w_mine, dst, az_ssem.at[s], az_rsem.at[z % 2], dev(x, y, (z + s) % NZ, c)
            ).start()

    w0_mine = w0.at[x, y]
    w1_mine = w1.at[y, x]

    @pl.when(jnp.logical_and(root, z % 2 == 0))
    def _():
        spread_z(w0_mine)

    @pl.when(jnp.logical_and(root, z % 2 == 1))
    def _():
        spread_z(w1_mine)

    dest = dest_ref[...]
    dsend[...] = jnp.broadcast_to(dest, (8, TOK))

    @pl.loop(1, NF)
    def _(s):
        rcopy(dsend, drecv.at[f], d_ssem.at[s], d_rsem.at[f], (dp, (f + s) % NF)).start()

    drecv[f] = dsend[...]

    dest_f = dest.astype(F32)
    owner = fdiv(dest_f, OWN)
    row_i = iota((TOK, TOK), 0)
    col_i = iota((TOK, TOK), 1)
    owner_col = jnp.sum(
        jnp.where(row_i == col_i, jnp.broadcast_to(owner, (TOK, TOK)), 0.0),
        axis=1, keepdims=True,
    )
    ahead = jnp.where(jnp.logical_and(owner_col == owner, row_i < col_i), 1.0, 0.0)
    position = owner * CAP + jnp.sum(ahead, axis=0, keepdims=True)
    p_col = iota((NF * 4 * CAP, 1), 0)
    p_owner = fdiv(p_col, 4 * CAP)
    p_in = p_col - p_owner * (4 * CAP)
    p_quarter = fdiv(p_in, CAP)
    p_rank = p_in - p_quarter * CAP
    p_pos = p_owner * CAP + p_rank
    picks = jnp.concatenate(
        [
            jnp.where(jnp.where(p_quarter == k, p_pos, -1.0) == position, 1.0, 0.0).astype(BF16)
            for k in range(4)
        ],
        axis=1,
    )
    loads[0].wait()
    stacked = jnp.concatenate([cot_v[:, QD * k : QD * (k + 1)] for k in range(4)], axis=0)
    packed[...] = dot_nn(picks, stacked).astype(BF16).reshape(NF, 4 * CAP, QD)

    @pl.loop(1, NF)
    def _(s):
        to = (f + s) % NF
        rcopy(packed.at[to], arrived.at[f], c_ssem.at[s], c_rsem.at[f], (dp, to)).start()

    arrived[f] = packed[f]

    @pl.when(root)
    def _():
        pltpu.make_async_copy(w_mine, w0_mine, own_sem).wait()

    @pl.when(z != 4 * c + 2 * h)
    def _():
        rcopy(w0_mine, w0_mine, az_ssem.at[0], az_rsem.at[0], sibling).wait_recv()

    for s in range(1, 4):
        rcopy(
            w0_mine, w0_mine, a1_ssem.at[0, s], a1_rsem.at[0, y], dev(x, (y + s) % NY, z, c)
        ).start()

    @pl.when(z != 4 * c + 2 * h + 1)
    def _():
        rcopy(w1_mine, w1_mine, az_ssem.at[0], az_rsem.at[1], sibling).wait_recv()

    for s in range(1, 4):
        rcopy(
            w1_mine, w1_mine, a1_ssem.at[1, s], a1_rsem.at[1, x], dev((x + s) % NX, y, z, c)
        ).start()

    for load in loads[1:]:
        load.wait()
    ids = ids_ref[...].astype(F32)
    srow = iota((OWN, OWN), 0)
    scol = iota((OWN, OWN), 1)
    ids_col = jnp.sum(
        jnp.where(srow == scol, jnp.broadcast_to(ids, (OWN, OWN)), 0.0), axis=1, keepdims=True
    )
    same_v[...] = jnp.where(ids_col == ids, 0.0, -1e30)
    lane = lax.broadcasted_iota(jnp.int32, (1, 128), 1)
    head_masks = (
        jnp.where(lane < 64, 1.0, 0.0).astype(BF16),
        jnp.where(lane < 64, 0.0, 1.0).astype(BF16),
    )
    first_head = lax.broadcasted_iota(jnp.int32, (OWN, 128), 1) < 64

    def forward(p):
        at = pl.ds(pl.multiple_of(p * 128, 128), 128)
        qp, kp, vp = q_v[:, at], k_v[:, at], v_v[:, at]
        outs = []
        for i in range(2):
            scores = dot_nt(qp * head_masks[i], kp) * SCALE
            scores = jnp.where(same_v[...] == 0.0, scores, -1e30)
            top = jnp.max(scores, axis=1, keepdims=True)
            e = jnp.exp(scores - top)
            prob = e * (1.0 / jnp.sum(e, axis=1, keepdims=True))
            probs[2 * p + i] = prob
            outs.append(dot_nn(prob.astype(BF16), vp))
        att[p] = jnp.where(first_head, outs[0], outs[1]).astype(BF16)

    pl.loop(0, PAIRS // 2)(forward)

    for s in range(1, 4):
        ys = (y + s) % NY
        rcopy(w0.at[x, ys], w0.at[x, ys], a1_ssem.at[0, s], a1_rsem.at[0, ys], sibling).wait_recv()
    for s in range(1, 4):
        rcopy(
            w0.at[x], w0.at[x], a2_ssem.at[0, s], a2_rsem.at[0, x], dev((x + s) % NX, y, z, c)
        ).start()
    for s in range(1, 4):
        xs = (x + s) % NX
        rcopy(w1.at[y, xs], w1.at[y, xs], a1_ssem.at[1, s], a1_rsem.at[1, xs], sibling).wait_recv()
    for s in range(1, 4):
        rcopy(
            w1.at[y], w1.at[y], a2_ssem.at[1, s], a2_rsem.at[1, y], dev(x, (y + s) % NY, z, c)
        ).start()

    pl.loop(PAIRS // 2, PAIRS)(forward)

    half = pl.ds(5 * c, 5)
    other = pl.ds(5 * (1 - c), 5)
    att_copy = rcopy(att.at[other], att_all.at[c], sib_ssem.at[0], sib_rsem.at[0], sibling)
    att_copy.start()
    att_all[c] = att[half]

    @pl.loop(1, NF)
    def _(s):
        frm = (f + s) % NF
        rcopy(dsend, drecv.at[frm], d_ssem.at[s], d_rsem.at[frm], sibling).wait_recv()

    dests = jnp.concatenate([drecv[k][0:1] for k in range(NF)], axis=0).astype(F32)
    owners = fdiv(dests, OWN)
    here = owners == f.astype(F32)
    before = jnp.where(row_i < col_i, 1.0, 0.0).astype(BF16)
    ranks = dot_nn(jnp.where(here, 1.0, 0.0).astype(BF16), before)
    ranks = jnp.where(here, ranks, -1.0).astype(BF16)
    slots = (dests - owners * OWN).astype(BF16)
    source = jnp.where(p_owner == iota((NF * 4 * CAP, NF), 1), 1.0, 0.0).astype(BF16)
    slot_col = jnp.sum(
        jnp.where(dot_nn(source, ranks) == p_rank, dot_nn(source, slots) + 1.0, 0.0),
        axis=1, keepdims=True,
    )
    slot_lane = iota((NF * 4 * CAP, OWN), 1) + 1.0

    @pl.loop(1, NF)
    def _(s):
        frm = (f + s) % NF
        rcopy(
            packed.at[frm], arrived.at[frm], c_ssem.at[s], c_rsem.at[frm], sibling
        ).wait_recv()

    rows_in = arrived[...].reshape(NF * 4 * CAP, QD)
    for k in range(4):
        place = jnp.where(
            jnp.where(p_quarter == k, slot_col, 0.0) == slot_lane, 1.0, 0.0
        ).astype(BF16)
        c_all[c, :, QD * k : QD * (k + 1)] = dot_tn(place, rows_in).astype(BF16)
    c_copy = rcopy(c_all.at[c], c_all.at[c], sib_ssem.at[1], sib_rsem.at[1], sibling)
    c_copy.start()
    rcopy(att.at[other], att_all.at[1 - c], sib_ssem.at[0], sib_rsem.at[0], sibling).wait_recv()
    att_t[...] = jnp.concatenate(
        [jnp.concatenate([att_all[g, i] for i in range(5)], axis=1) for g in range(2)], axis=0
    ).T
    rcopy(
        c_all.at[1 - c], c_all.at[1 - c], sib_ssem.at[1], sib_rsem.at[1], sibling
    ).wait_recv()

    for s in (1, 2, 3, 0):
        xs = (x + s) % NX
        cols = c_all[:, :, pl.ds(pl.multiple_of(xs * QD, 128), QD)].reshape(2 * OWN, QD)
        share = dot_nn(att_t[...], cols)
        for ys in range(NY):
            n = row_of(ys, 0)
            s0[xs, ys] = share[ROWS * n : ROWS * (n + 1)].astype(BF16)
            n = row_of(ys, 1)
            s1[ys, xs] = share[ROWS * n : ROWS * (n + 1)].astype(BF16)
        if s:
            rcopy(
                s0.at[xs], r0.at[x], b2_ssem.at[0, s], b2_rsem.at[0, x], dev(xs, y, z, c)
            ).start()
    for s in range(1, 4):
        ys = (y + s) % NY
        rcopy(
            s1.at[ys], r1.at[y], b2_ssem.at[1, s], b2_rsem.at[1, y], dev(x, ys, z, c)
        ).start()

    for s in range(1, 4):
        xs, ys = (x + s) % NX, (y + s) % NY
        rcopy(w0.at[xs], w0.at[xs], a2_ssem.at[0, s], a2_rsem.at[0, xs], sibling).wait_recv()
        rcopy(w1.at[ys], w1.at[ys], a2_ssem.at[1, s], a2_rsem.at[1, ys], sibling).wait_recv()
    total = None
    for k in range(4):
        blocks = []
        for n in range(8):
            ys, j = 2 * (n // 4) + n % 2, (n // 2) % 2
            blocks.append(w0[k, ys] if j == 0 else w1[ys, k])
        wk = jnp.concatenate(blocks, axis=0)
        cols = c_all[:, :, QD * k : QD * (k + 1)].reshape(2 * OWN, QD)
        term = dot_nt(cols, wk)
        total = term if total is None else total + term
    total = total.astype(BF16)
    for g in range(2):
        for i in range(5):
            g_tmp[g, i] = total[OWN * g : OWN * (g + 1), 128 * i : 128 * (i + 1)]
    g_copy = rcopy(g_tmp.at[1 - c], g_v.at[half], sib_ssem.at[2], sib_rsem.at[2], sibling)
    g_copy.start()
    g_v[half] = g_tmp[c]

    live = ids_col >= 0.0

    def backward(p):
        at = pl.ds(pl.multiple_of(p * 128, 128), 128)
        qp, kp, vp = q_v[:, at], k_v[:, at], v_v[:, at]
        gp = g_v[p]
        dqs, dks, dvs = [], [], []
        for i in range(2):
            prob = probs[2 * p + i]
            dvs.append(dot_tn(prob.astype(BF16), gp))
            pg = dot_nt(gp * head_masks[i], vp)
            delta = jnp.sum(prob * pg, axis=1, keepdims=True)
            sg = (prob * (pg - delta)).astype(BF16)
            dqs.append(dot_nn(sg, kp))
            dks.append(dot_tn(sg, qp))

        def put(ref, parts, scale):
            value = jnp.where(first_head, parts[0], parts[1]) * scale
            ref[:, at] = jnp.where(live, value, 0.0).astype(BF16)

        put(dq_v, dqs, SCALE)
        put(dk_v, dks, SCALE)
        put(dv_v, dvs, 1.0)

    mine_first = 5 * c
    pl.loop(0, PAIRS // 2)(lambda i: backward(mine_first + i))
    rcopy(
        g_tmp.at[1 - c], g_v.at[other], sib_ssem.at[2], sib_rsem.at[2], sibling
    ).wait_recv()
    theirs_first = 5 * (1 - c)
    pl.loop(0, PAIRS // 2)(lambda i: backward(theirs_first + i))
    outs = [
        pltpu.make_async_copy(src, dst, out_sem.at[i])
        for i, (src, dst) in enumerate(((dq_v, dq_hbm), (dk_v, dk_hbm), (dv_v, dv_hbm)))
    ]
    for out in outs:
        out.start()

    for s in range(1, 4):
        xs = (x + s) % NX
        rcopy(s0.at[xs], r0.at[xs], b2_ssem.at[0, s], b2_rsem.at[0, xs], sibling).wait_recv()
    for s in (1, 2, 3, 0):
        ys = (y + s) % NY
        acc = s0[x, ys].astype(F32)
        for e in range(1, 4):
            acc += r0[(x + e) % NX, ys].astype(F32)
        t0[ys] = acc.astype(BF16)
        if s:
            rcopy(
                t0.at[ys], u0.at[y], b1_ssem.at[0, s], b1_rsem.at[0, y], dev(x, ys, z, c)
            ).start()
        else:
            vf[0] = acc
    for s in range(1, 4):
        ys = (y + s) % NY
        rcopy(s1.at[ys], r1.at[ys], b2_ssem.at[1, s], b2_rsem.at[1, ys], sibling).wait_recv()
    for s in (1, 2, 3, 0):
        xs = (x + s) % NX
        acc = s1[y, xs].astype(F32)
        for e in range(1, 4):
            acc += r1[(y + e) % NY, xs].astype(F32)
        t1[xs] = acc.astype(BF16)
        if s:
            rcopy(
                t1.at[xs], u1.at[x], b1_ssem.at[1, s], b1_rsem.at[1, x], dev(xs, y, z, c)
            ).start()
        else:
            vf[1] = acc

    for j, (me, src, dst) in enumerate(((y, t0, u0), (x, t1, u1))):
        acc = vf[j]
        for s in range(1, 4):
            frm = (me + s) % 4
            rcopy(
                src.at[frm], dst.at[frm], b1_ssem.at[j, s], b1_rsem.at[j, frm], sibling
            ).wait_recv()
            acc += dst[frm].astype(F32)
        vf[j] = acc
        vb[j] = acc.astype(BF16)
        z_root = 4 * c + 2 * h + j

        @pl.when(z != z_root)
        def _(j=j, z_root=z_root):
            rcopy(
                vb.at[j], zr.at[z], bz_ssem.at[j], bz_rsem.at[z], dev(x, y, z_root, c)
            ).start()

    def emit(i):
        pltpu.make_async_copy(
            fall.at[i],
            wg_hbm.at[:, pl.ds(pl.multiple_of(i * QD, 128), QD)],
            wg_sem.at[i],
        ).start()

    y_twin = (y + 2) % NY

    @pl.when(root)
    def _():
        acc = vf[z % 2]
        for s in range(1, NZ):
            frm = (z + s) % NZ
            rcopy(vb.at[0], zr.at[frm], bz_ssem.at[0], bz_rsem.at[frm], sibling).wait_recv()
            acc += zr[frm].astype(F32)
        fall[x] = acc
        rcopy(fall.at[x], fall.at[x], f1_ssem, f1_rsem, dev(x, y_twin, z, c)).start()

    @pl.when(jnp.logical_and(active, (z % 4) // 2 != h))
    def _():
        rcopy(fall.at[x], fall.at[x], f1_ssem, f1_rsem, sibling).wait_recv()

    @pl.when(active)
    def _():
        for s in range(1, 4):
            rcopy(
                fall.at[x], fall.at[x], f2_ssem.at[s], f2_rsem.at[x], dev((x + s) % NX, y, z, c)
            ).start()
        for s in range(4):
            xs = (x + s) % NX
            if s:
                rcopy(
                    fall.at[xs], fall.at[xs], f2_ssem.at[s], f2_rsem.at[xs], sibling
                ).wait_recv()
            rcopy(fall.at[xs], fall.at[xs], f3_ssem.at[xs], f3_rsem.at[xs], sibling).start()
            emit(xs)

    @pl.when(jnp.logical_not(active))
    def _():
        for s in range(4):
            xs = (x + s) % NX
            rcopy(
                fall.at[xs], fall.at[xs], f3_ssem.at[xs], f3_rsem.at[xs], sibling
            ).wait_recv()
            emit(xs)

    @pl.when(root)
    def _():
        @pl.loop(1, NZ)
        def _(s):
            rcopy(w_mine, w0_mine, az_ssem.at[s], az_rsem.at[0], sibling).wait_send()

        rcopy(fall.at[x], fall.at[x], f1_ssem, f1_rsem, sibling).wait_send()

    @pl.loop(1, NF)
    def _(s):
        rcopy(dsend, drecv.at[f], d_ssem.at[s], d_rsem.at[f], sibling).wait_send()
        rcopy(packed.at[f], arrived.at[f], c_ssem.at[s], c_rsem.at[f], sibling).wait_send()

    for s in range(1, 4):
        for j, w in enumerate((w0_mine, w1_mine)):
            rcopy(w, w, a1_ssem.at[j, s], a1_rsem.at[j, 0], sibling).wait_send()
        for j, w in enumerate((w0.at[x], w1.at[y])):
            rcopy(w, w, a2_ssem.at[j, s], a2_rsem.at[j, 0], sibling).wait_send()
        for j, w in enumerate((s0.at[x], s1.at[y])):
            rcopy(w, w, b2_ssem.at[j, s], b2_rsem.at[j, 0], sibling).wait_send()
        for j, w in enumerate((t0.at[y], t1.at[x])):
            rcopy(w, w, b1_ssem.at[j, s], b1_rsem.at[j, 0], sibling).wait_send()
    att_copy.wait_send()
    c_copy.wait_send()
    g_copy.wait_send()
    for j in range(2):

        @pl.when(z != 4 * c + 2 * h + j)
        def _(j=j):
            rcopy(vb.at[j], zr.at[z], bz_ssem.at[j], bz_rsem.at[z], sibling).wait_send()

    @pl.when(active)
    def _():
        for s in range(1, 4):
            rcopy(fall.at[x], fall.at[x], f2_ssem.at[s], f2_rsem.at[x], sibling).wait_send()
        for s in range(4):
            rcopy(fall.at[s], fall.at[s], f3_ssem.at[s], f3_rsem.at[s], sibling).wait_send()

    for out in outs:
        out.wait()
    for i in range(4):
        pltpu.make_async_copy(
            fall.at[i], wg_hbm.at[:, QD * i : QD * (i + 1)], wg_sem.at[i]
        ).wait()


def per_device(cotangent, out_weight, queries, key_vectors, value_vectors, destination, protein_ids):
    dma = pltpu.SemaphoreType.DMA
    vmem = pltpu.VMEM
    slots = jax.ShapeDtypeStruct((OWN, PAIRS * 128), BF16)
    any_space = pl.BlockSpec(memory_space=pl.ANY)
    in_vmem = pl.BlockSpec(memory_space=pltpu.VMEM)
    return pl.pallas_call(
        kernel,
        out_shape=(slots, slots, slots, jax.ShapeDtypeStruct((ROWS, D), F32)),
        in_specs=[any_space] * 5 + [in_vmem] * 2,
        out_specs=(any_space,) * 4,
        scratch_shapes=[
            vmem((TOK, D), BF16),
            *[vmem((OWN, PAIRS * 128), BF16) for _ in range(6)],
            vmem((8, TOK), jnp.int32),
            vmem((NF, 8, TOK), jnp.int32),
            vmem((NF, 4 * CAP, QD), BF16),
            vmem((NF, 4 * CAP, QD), BF16),
            vmem((2, OWN, D), BF16),
            vmem((PAIRS, OWN, 128), BF16),
            vmem((2, 5, OWN, 128), BF16),
            vmem((640, 2 * OWN), BF16),
            vmem((2 * PAIRS, OWN, OWN), F32),
            vmem((OWN, OWN), F32),
            vmem((NX, NY, ROWS, QD), BF16),
            vmem((NY, NX, ROWS, QD), BF16),
            vmem((2, 5, OWN, 128), BF16),
            vmem((PAIRS, OWN, 128), BF16),
            *[vmem((4, 4, ROWS, QD), BF16) for _ in range(4)],
            *[vmem((4, ROWS, QD), BF16) for _ in range(4)],
            vmem((2, ROWS, QD), F32),
            vmem((2, ROWS, QD), BF16),
            vmem((NZ, ROWS, QD), BF16),
            vmem((NX, ROWS, QD), F32),
            dma((4,)), dma((3,)), dma((4,)), dma,
            dma((NF,)), dma((NF,)), dma((NF,)), dma((NF,)),
            dma((NZ,)), dma((2,)), dma((2, 4)), dma((2, 4)), dma((2, 4)), dma((2, 4)),
            dma((3,)), dma((3,)),
            dma((2, 4)), dma((2, 4)), dma((2, 4)), dma((2, 4)), dma((2,)), dma((NZ,)),
            dma, dma, dma((4,)), dma((4,)), dma((4,)), dma((4,)),
        ],
        compiler_params=pltpu.CompilerParams(
            collective_id=0, has_side_effects=True, vmem_limit_bytes=56 * 1024 * 1024
        ),
    )(
        cotangent, out_weight, queries, key_vectors, value_vectors,
        destination.reshape(1, TOK), protein_ids.reshape(1, OWN),
    )


def solution(mesh):
    rows = P(("dp", "fsdp"), None)
    return jax.shard_map(
        per_device,
        mesh=mesh,
        in_specs=(rows, P("fsdp", None), rows, rows, rows, P(("dp", "fsdp")), P(("dp", "fsdp"))),
        out_specs=(rows, rows, rows, P("fsdp", None)),
        check_vma=False,
    )
```

time: 612 us -> 110 us (0.18)
  the two profiles are of different devices: /device:TPU:1 before, /device:TPU:49 now
where the time goes in v1:
time: 110 us
  Pallas kernels  105 us (95%)
  local copies, waits for them, and re-layouts  4.38 us (4%)
    pallas_call x1, Pallas kernels, per_device(): pl.pallas_call(kernel, out_shape=(slots, slots, slots, jax.ShapeDtypeStru...  105 us
    unnamed x10, local copies, waits for them, and re-layouts  4.38 us

profile of v1, /device:TPU:49, one launch (start us, length us, event | category | flops | bytes accessed | tf_op | source)
XLA Modules:
  0.0 109.9 jit_solution(7928448155924884195)
XLA Ops:
  0.6 104.8 %shard_map.102 = (bf16[192,1280]{1,0:T(8,128)(2,1)}, bf16[192,1280]{1,0:T(8,128)(2,1)}, bf16[192,1280]{1,0:T(8,128)(2,1)}, f32[80,2560]{1,0:T(8,128)}) custom-call(bf16[128,2560]{1,0:T(8,128)(2,1)} %cot_hbm.1, bf16[80,2560]{1,0:T(8,128)(2,1)} %w_hbm.1, bf16[192,1280]{1,0:T(8,128)(2,1)} %q_hbm.1, bf16[192,1280]{1,0:T(8,128)(2,1)} %k_hbm.1, ...), custom_call_target="tpu_custom_call" | custom-call | tf_op jit(solution)/shard_map/pallas_call | solution.py:521
  105.5 0.0 copy-start.2
  105.5 0.0 copy-start.1
  105.5 1.9 %copy.15 = bf16[192,1280]{1,0:T(8,128)(2,1)} copy(bf16[192,1280]{1,0:T(8,128)(2,1)} %get-tuple-element.8) | data formatting | bytes 983040
  107.4 0.0 copy-done.2
  107.4 0.0 copy-start
  107.4 0.8 copy.16
  108.2 0.0 copy-done.1
  108.2 0.8 copy.17
  109.0 0.0 copy-done
  109.0 0.9 copy.18
Async XLA Ops:
  105.5 1.9 %copy-start.2 = (bf16[192,1280]{1,0:T(8,128)(2,1)S(1)}, bf16[192,1280]{1,0:T(8,128)(2,1)}, u32[]{:S(2)}) copy-start(bf16[192,1280]{1,0:T(8,128)(2,1)} %get-tuple-element.9) | copy-start | bytes 1474564
  105.5 2.7 %copy-start.1 = (bf16[192,1280]{1,0:T(8,128)(2,1)S(1)}, bf16[192,1280]{1,0:T(8,128)(2,1)}, u32[]{:S(2)}) copy-start(bf16[192,1280]{1,0:T(8,128)(2,1)} %get-tuple-element.10) | copy-start | bytes 1474564
  107.4 1.6 %copy-start = (f32[80,2560]{1,0:T(8,128)S(1)}, f32[80,2560]{1,0:T(8,128)}, u32[]{:S(2)}) copy-start(f32[80,2560]{1,0:T(8,128)} %get-tuple-element.11) | copy-start | bytes 2457604

commit v2 on v1

v2 whole, which is shorter than its diff:
```python
import jax
import jax.numpy as jnp
from jax import lax
from jax.experimental import pallas as pl
from jax.experimental.pallas import tpu as pltpu
from jax.sharding import PartitionSpec as P

F32 = jnp.float32
BF16 = jnp.bfloat16
MESH = pl.DeviceIdType.MESH

NX, NY, NZ, NF = 4, 4, 8, 16
TOK = 128
OWN = 192
CAP = 12
D = 2560
QD = D // 4
ROWS = 80
BLK = 64
SPAD = 256
PAIRS = 10
SCALE = 0.125


def fdiv(values, by):
    return jnp.floor((values + 0.5) * (1.0 / by))


def iota(shape, dim):
    return lax.broadcasted_iota(jnp.int32, shape, dim).astype(F32)


def dot_nt(a, b):
    return lax.dot_general(a, b, (((1,), (1,)), ((), ())), preferred_element_type=F32)


def dot_tn(a, b):
    return lax.dot_general(a, b, (((0,), (0,)), ((), ())), preferred_element_type=F32)


def dot_nn(a, b):
    return jnp.dot(a, b, preferred_element_type=F32)


def row_of(y, j):
    return 4 * j + y


def kernel(
    cot_hbm, w_hbm, q_hbm, k_hbm, v_hbm, dest_ref, ids_ref,
    dq_hbm, dk_hbm, dv_hbm, wg_hbm,
    q_v, k_v, v_v, dq_v, dk_v, dv_v,
    dsend, drecv, c_all, h_own, h_tok,
    att, att_out, att_in, att_t, att_all, probs, same_v,
    w0, w1, g_tmp, g_tok, g_out, g_in, g_v,
    s0, s1, r0, r1, t0, t1, u0, u1, vf, vb, zr, fall,
    load_sem, out_sem, wg_sem, own_sem,
    d_ssem, d_rsem, c_ssem, c_rsem, g_ssem, g_rsem,
    az_ssem, az_rsem, a1_ssem, a1_rsem, a2_ssem, a2_rsem,
    sib_ssem, sib_rsem,
    b2_ssem, b2_rsem, b1_ssem, b1_rsem, bz_ssem, bz_rsem,
    f2_ssem, f2_rsem, f3_ssem, f3_rsem,
):
    dp = lax.axis_index("dp")
    f = lax.axis_index("fsdp")
    c = dp % 2
    x = (dp // 2) % NX
    h = dp // 8
    z = f // 2
    y = 2 * h + f % 2
    o = 1 - c

    def dev(x_, y_, z_, c_):
        return (((y_ // 2) * NX + x_) * 2 + c_, z_ * 2 + y_ % 2)

    def rcopy(src, dst, ssem, rsem, target):
        return pltpu.make_async_remote_copy(
            src_ref=src, dst_ref=dst, send_sem=ssem, recv_sem=rsem,
            device_id=target, device_id_type=MESH,
        )

    sibling = dev(x, y, z, o)

    loads = [
        pltpu.make_async_copy(src, dst, load_sem.at[i])
        for i, (src, dst) in enumerate(
            ((q_hbm, q_v), (k_hbm, k_v), (v_hbm, v_v), (cot_hbm, c_all.at[c]))
        )
    ]
    for load in loads:
        load.start()

    barrier = pltpu.get_barrier_semaphore()

    @pl.loop(1, NF)
    def _(s):
        pl.semaphore_signal(
            barrier, inc=1, device_id=(dp, (f + s) % NF), device_id_type=MESH
        )

    for s in range(1, 4):
        pl.semaphore_signal(
            barrier, inc=1, device_id=dev((x + s) % NX, y, z, c), device_id_type=MESH
        )
        pl.semaphore_signal(
            barrier, inc=1, device_id=dev(x, (y + s) % NY, z, c), device_id_type=MESH
        )
        pl.semaphore_signal(
            barrier, inc=1, device_id=dev((x + s) % NX, (y + 2) % NY, z, c), device_id_type=MESH
        )
    pl.semaphore_signal(barrier, inc=1, device_id=sibling, device_id_type=MESH)

    ids = ids_ref[...].astype(F32)
    srow = iota((OWN, OWN), 0)
    scol = iota((OWN, OWN), 1)
    ids_col = jnp.sum(
        jnp.where(srow == scol, jnp.broadcast_to(ids, (OWN, OWN)), 0.0), axis=1, keepdims=True
    )
    same_v[...] = jnp.where(ids_col == ids, 1.0, 0.0)
    dest = dest_ref[...]
    dsend[...] = jnp.broadcast_to(dest, (8, TOK))
    att[:, OWN:SPAD] = jnp.zeros((PAIRS, SPAD - OWN, 128), BF16)
    lane = lax.broadcasted_iota(jnp.int32, (1, 128), 1)
    head_masks = (
        jnp.where(lane < 64, 1.0, 0.0).astype(BF16),
        jnp.where(lane < 64, 0.0, 1.0).astype(BF16),
    )
    first_head = lax.broadcasted_iota(jnp.int32, (OWN, 128), 1) < 64

    pl.semaphore_wait(barrier, 25)

    @pl.loop(1, NF)
    def _(s):
        rcopy(dsend, drecv.at[f], d_ssem.at[s], d_rsem.at[f], (dp, (f + s) % NF)).start()

    drecv[f] = dsend[...]

    active = z // 4 == c
    root = jnp.logical_and(active, z % 2 == h)
    root_j = (z % 4) // 2
    w_mine = w_hbm.at[:, pl.ds(pl.multiple_of(x * QD, 128), QD)]

    def spread_z(dst):
        pltpu.make_async_copy(w_mine, dst, own_sem).start()

        @pl.loop(1, NZ)
        def _(s):
            rcopy(
                w_mine, dst, az_ssem.at[s], az_rsem.at[root_j], dev(x, y, (z + s) % NZ, c)
            ).start()

    w0_mine = w0.at[x, y]
    w1_mine = w1.at[y, x]

    @pl.when(jnp.logical_and(root, root_j == 0))
    def _():
        spread_z(w0_mine)

    @pl.when(jnp.logical_and(root, root_j == 1))
    def _():
        spread_z(w1_mine)

    c_copy = rcopy(cot_hbm, c_all.at[c], sib_ssem.at[1], sib_rsem.at[1], sibling)
    c_copy.start()

    def both_heads(rows):
        return jnp.concatenate([rows * head_masks[0], rows * head_masks[1]], axis=0)

    def forward(p):
        at = pl.ds(pl.multiple_of(p * 128, 128), 128)
        qp, kp, vp = q_v[:, at], k_v[:, at], v_v[:, at]
        scores = dot_nt(both_heads(qp), kp) * SCALE
        same = jnp.concatenate([same_v[...], same_v[...]], axis=0)
        scores = jnp.where(same > 0.0, scores, -1e30)
        top = jnp.max(scores, axis=1, keepdims=True)
        e = jnp.exp(scores - top)
        prob = e * (1.0 / jnp.sum(e, axis=1, keepdims=True))
        probs[p] = prob
        out = dot_nn(prob.astype(BF16), vp)
        att[p, 0:OWN] = jnp.where(first_head, out[:OWN], out[OWN:]).astype(BF16)

    for load in loads[:3]:
        load.wait()
    pl.loop(0, 5)(lambda i: forward(5 * o + i))

    @pl.loop(1, NF)
    def _(s):
        frm = (f + s) % NF
        rcopy(dsend, drecv.at[frm], d_ssem.at[s], d_rsem.at[frm], sibling).wait_recv()

    row_i = iota((TOK, TOK), 0)
    col_i = iota((TOK, TOK), 1)
    p_col = iota((NF * BLK, 1), 0)
    p_dev = fdiv(p_col, BLK)
    p_in = p_col - p_dev * BLK
    p_pair = fdiv(p_in, CAP)
    p_rank = p_in - p_pair * CAP
    dests = jnp.concatenate([drecv[k][0:1] for k in range(NF)], axis=0).astype(F32)
    owners = fdiv(dests, OWN)
    here = owners == f.astype(F32)
    before = jnp.where(row_i < col_i, 1.0, 0.0).astype(BF16)
    ranks = dot_nn(jnp.where(here, 1.0, 0.0).astype(BF16), before)
    ranks = jnp.where(here, ranks, -1.0).astype(BF16)
    slots = (dests - owners * OWN).astype(BF16)
    source = jnp.where(p_dev == iota((NF * BLK, NF), 1), 1.0, 0.0).astype(BF16)
    slot_col = jnp.sum(
        jnp.where(dot_nn(source, ranks) == p_rank, dot_nn(source, slots) + 1.0, 0.0),
        axis=1, keepdims=True,
    )
    slot_lane = iota((1, SPAD), 1) + 1.0
    for k in range(5):
        h_own[:, SPAD * k : SPAD * (k + 1)] = jnp.where(
            jnp.where(p_pair == k, slot_col, 0.0) == slot_lane, 1.0, 0.0
        ).astype(BF16)

    def send_att(n, part):
        rows = att[pl.ds(5 * part, 5)].reshape(5 * SPAD, 128)
        att_out[n] = dot_nn(h_own[...], rows).astype(BF16).reshape(NF, BLK, 128)

        @pl.loop(1, NF)
        def _(s):
            to = (f + s) % NF
            rcopy(
                att_out.at[n, to], att_in.at[n, f], c_ssem.at[n, s], c_rsem.at[n, f], (dp, to)
            ).start()

        att_in[n, f] = att_out[n, f]

    send_att(0, o)

    pl.loop(0, 2)(lambda i: forward(5 * c + i))

    def pass_on(j, k):
        for s in (1, 3, 2):
            ref = w0.at[x, k] if j == 0 else w1.at[y, k]
            to = dev((x + s) % NX, y, z, c) if j == 0 else dev(x, (y + s) % NY, z, c)
            me = x if j == 0 else y
            rcopy(ref, ref, a2_ssem.at[j, s, k], a2_rsem.at[j, me, k], to).start()

    @pl.when(root)
    def _():
        pltpu.make_async_copy(w_mine, w0_mine, own_sem).wait()

    @pl.when(z != 4 * c + h)
    def _():
        rcopy(w0_mine, w0_mine, az_ssem.at[0], az_rsem.at[0], sibling).wait_recv()

    for s in (1, 3, 2):
        rcopy(
            w0_mine, w0_mine, a1_ssem.at[0, s], a1_rsem.at[0, y], dev(x, (y + s) % NY, z, c)
        ).start()
    pass_on(0, y)

    @pl.when(z != 4 * c + 2 + h)
    def _():
        rcopy(w1_mine, w1_mine, az_ssem.at[0], az_rsem.at[1], sibling).wait_recv()

    for s in (1, 3, 2):
        rcopy(
            w1_mine, w1_mine, a1_ssem.at[1, s], a1_rsem.at[1, x], dev((x + s) % NX, y, z, c)
        ).start()
    pass_on(1, x)

    pl.loop(2, 5)(lambda i: forward(5 * c + i))
    send_att(1, c)

    dest_f = dest.astype(F32)
    owner = fdiv(dest_f, OWN)
    owner_col = jnp.sum(
        jnp.where(row_i == col_i, jnp.broadcast_to(owner, (TOK, TOK)), 0.0),
        axis=1, keepdims=True,
    )
    ahead = jnp.where(jnp.logical_and(owner_col == owner, row_i < col_i), 1.0, 0.0)
    position = owner * CAP + jnp.sum(ahead, axis=0, keepdims=True)
    p_pos = p_dev * CAP + p_rank
    for k in range(5):
        h_tok[:, TOK * k : TOK * (k + 1)] = jnp.where(
            jnp.where(p_pair == k, p_pos, -1.0) == position, 1.0, 0.0
        ).astype(BF16)

    for s in (1, 3, 2):
        ys, xs = (y + s) % NY, (x + s) % NX
        rcopy(w0.at[x, ys], w0.at[x, ys], a1_ssem.at[0, s], a1_rsem.at[0, ys], sibling).wait_recv()
        pass_on(0, ys)
        rcopy(w1.at[y, xs], w1.at[y, xs], a1_ssem.at[1, s], a1_rsem.at[1, xs], sibling).wait_recv()
        pass_on(1, xs)

    def take_att(n):
        @pl.loop(1, NF)
        def _(s):
            frm = (f + s) % NF
            rcopy(
                att_out.at[n, frm], att_in.at[n, frm], c_ssem.at[n, s], c_rsem.at[n, frm], sibling
            ).wait_recv()

        out = dot_tn(att_in[n].reshape(NF * BLK, 128), h_tok[...]).astype(BF16)
        return jnp.concatenate([out[:, TOK * k : TOK * (k + 1)] for k in range(5)], axis=0)

    att_t[...] = take_att(0)
    att_copy = rcopy(att_t, att_all.at[c], sib_ssem.at[0], sib_rsem.at[0], sibling)
    att_copy.start()
    att_all[c] = take_att(1)
    loads[3].wait()
    rcopy(cot_hbm, c_all.at[o], sib_ssem.at[1], sib_rsem.at[1], sibling).wait_recv()
    rcopy(att_t, att_all.at[o], sib_ssem.at[0], sib_rsem.at[0], sibling).wait_recv()

    def share_out(j, to, k):
        if j == 0:
            src, dst, me, device = s0.at[to, k], r0.at[x, k], x, dev(to, y, z, c)
        else:
            src, dst, me, device = s1.at[to, k], r1.at[y, k], y, dev(x, to, z, c)
        rcopy(src, dst, b2_ssem.at[j, to, k], b2_rsem.at[j, me, k], device).start()

    att_both = jnp.concatenate([att_all[0], att_all[1]], axis=1)
    for s in (1, 2, 3, 0):
        xs = (x + s) % NX
        cols = c_all[:, :, pl.ds(pl.multiple_of(xs * QD, 128), QD)].reshape(2 * TOK, QD)
        share = dot_nn(att_both, cols)
        for ys in range(NY):
            n = row_of(ys, 0)
            s0[xs, ys] = share[ROWS * n : ROWS * (n + 1)].astype(BF16)
            n = row_of(ys, 1)
            s1[ys, xs] = share[ROWS * n : ROWS * (n + 1)].astype(BF16)
        if s:
            share_out(0, xs, (y + 1) % NY)
        for e in (1, 3, 2):
            share_out(1, (y + e) % NY, xs)
    for e in (2, 3, 0):
        for s in (1, 3, 2):
            share_out(0, (x + s) % NX, (y + e) % NY)

    for s in range(1, 4):
        xs, ys = (x + s) % NX, (y + s) % NY
        for k in range(4):
            for j, ref, frm in ((0, w0.at[xs, k], xs), (1, w1.at[ys, k], ys)):
                rcopy(ref, ref, a2_ssem.at[j, s, k], a2_rsem.at[j, frm, k], sibling).wait_recv()
    total = None
    for k in range(4):
        blocks = []
        for n in range(8):
            ys, j = n % 4, n // 4
            blocks.append(w0[k, ys] if j == 0 else w1[ys, k])
        wk = jnp.concatenate(blocks, axis=0)
        cols = c_all[:, :, QD * k : QD * (k + 1)].reshape(2 * TOK, QD)
        term = dot_nt(cols, wk)
        total = term if total is None else total + term
    total = total.astype(BF16)
    for g in range(2):
        for i in range(5):
            g_tmp[g, i] = total[TOK * g : TOK * (g + 1), 128 * i : 128 * (i + 1)]
    g_copy = rcopy(g_tmp.at[o], g_tok, sib_ssem.at[2], sib_rsem.at[2], sibling)
    g_copy.start()

    def send_grad(n, rows):
        g_out[n] = dot_nn(h_tok[...], rows.reshape(5 * TOK, 128)).astype(BF16).reshape(NF, BLK, 128)

        @pl.loop(1, NF)
        def _(s):
            to = (f + s) % NF
            rcopy(
                g_out.at[n, to], g_in.at[n, f], g_ssem.at[n, s], g_rsem.at[n, f], (dp, to)
            ).start()

        g_in[n, f] = g_out[n, f]

    send_grad(0, g_tmp[c])
    rcopy(g_tmp.at[o], g_tok, sib_ssem.at[2], sib_rsem.at[2], sibling).wait_recv()
    send_grad(1, g_tok[...])

    for e in (1, 2, 3, 0):
        for j in range(2):
            if j == 0:
                own, ins, out, nxt, me, k = s0, r0, t0, u0, x, (y + e) % NY
                after, to = y, dev(x, k, z, c)
            else:
                own, ins, out, nxt, me, k = s1, r1, t1, u1, y, (x + e) % NX
                after, to = x, dev(k, y, z, c)
            acc = own[me, k].astype(F32)
            for s in (1, 3, 2):
                frm = (me + s) % 4
                rcopy(
                    own.at[frm, k], ins.at[frm, k], b2_ssem.at[j, 0, 0], b2_rsem.at[j, frm, k],
                    sibling,
                ).wait_recv()
                acc += ins[frm, k].astype(F32)
            if e:
                out[k] = acc.astype(BF16)
                rcopy(
                    out.at[k], nxt.at[after], b1_ssem.at[j, e], b1_rsem.at[j, after], to
                ).start()
            else:
                vf[j] = acc

    for j, (me, src, dst) in enumerate(((y, t0, u0), (x, t1, u1))):
        acc = vf[j]
        for s in range(1, 4):
            frm = (me + s) % 4
            rcopy(
                src.at[frm], dst.at[frm], b1_ssem.at[j, s], b1_rsem.at[j, frm], sibling
            ).wait_recv()
            acc += dst[frm].astype(F32)
        vf[j] = acc
        vb[j] = acc.astype(BF16)
        z_root = 4 * c + 2 * j + h

        @pl.when(z != z_root)
        def _(j=j, z_root=z_root):
            rcopy(
                vb.at[j], zr.at[z], bz_ssem.at[j], bz_rsem.at[z], dev(x, y, z_root, c)
            ).start()

    def take_grad(n):
        @pl.loop(1, NF)
        def _(s):
            frm = (f + s) % NF
            rcopy(
                g_out.at[n, frm], g_in.at[n, frm], g_ssem.at[n, s], g_rsem.at[n, frm], sibling
            ).wait_recv()

        out = dot_tn(g_in[n].reshape(NF * BLK, 128), h_own[...])
        for k in range(5):
            g_v[k] = out[:, SPAD * k : SPAD * (k + 1)].T[:OWN].astype(BF16)

    live = ids_col >= 0.0

    def backward(p, gp):
        at = pl.ds(pl.multiple_of(p * 128, 128), 128)
        qp, kp, vp = q_v[:, at], k_v[:, at], v_v[:, at]
        prob = probs[p]
        pg = dot_nt(both_heads(gp), vp)
        delta = jnp.sum(prob * pg, axis=1, keepdims=True)
        sg = (prob * (pg - delta)).astype(BF16)
        pb = prob.astype(BF16)
        dq = dot_nn(sg, kp)

        def put(ref, one, two, scale):
            value = jnp.where(first_head, one, two) * scale
            ref[:, at] = jnp.where(live, value, 0.0).astype(BF16)

        put(dq_v, dq[:OWN], dq[OWN:], SCALE)
        put(dk_v, dot_tn(sg[:OWN], qp), dot_tn(sg[OWN:], qp), SCALE)
        put(dv_v, dot_tn(pb[:OWN], gp), dot_tn(pb[OWN:], gp), 1.0)

    take_grad(0)
    pl.loop(0, 5)(lambda i: backward(5 * c + i, g_v[i]))
    take_grad(1)
    pl.loop(0, 5)(lambda i: backward(5 * o + i, g_v[i]))
    outs = [
        pltpu.make_async_copy(src, dst, out_sem.at[i])
        for i, (src, dst) in enumerate(((dq_v, dq_hbm), (dk_v, dk_hbm), (dv_v, dv_hbm)))
    ]
    for out in outs:
        out.start()

    def emit(i):
        pltpu.make_async_copy(
            fall.at[i],
            wg_hbm.at[:, pl.ds(pl.multiple_of(i * QD, 128), QD)],
            wg_sem.at[i],
        ).start()

    def to_sibling(i):
        rcopy(fall.at[i], fall.at[i], f3_ssem.at[i], f3_rsem.at[i], sibling).start()
        emit(i)

    @pl.when(root)
    def _():
        acc = vf[root_j]
        for s in range(1, NZ):
            frm = (z + s) % NZ
            rcopy(vb.at[0], zr.at[frm], bz_ssem.at[0], bz_rsem.at[frm], sibling).wait_recv()
            acc += zr[frm].astype(F32)
        fall[x] = acc.astype(BF16)
        for s in (1, 3, 2, 0):
            for e in (2, 0):
                if s or e:
                    rcopy(
                        fall.at[x], fall.at[x], f2_ssem.at[s, e // 2], f2_rsem.at[x],
                        dev((x + s) % NX, (y + e) % NY, z, c),
                    ).start()
        to_sibling(x)

    @pl.when(jnp.logical_and(active, z % 2 != h))
    def _():
        rcopy(fall.at[x], fall.at[x], f2_ssem.at[0, 0], f2_rsem.at[x], sibling).wait_recv()
        to_sibling(x)

    @pl.when(active)
    def _():
        for s in (1, 3, 2):
            xs = (x + s) % NX
            rcopy(fall.at[xs], fall.at[xs], f2_ssem.at[0, 0], f2_rsem.at[xs], sibling).wait_recv()
            to_sibling(xs)

    @pl.when(jnp.logical_not(active))
    def _():
        for s in (0, 1, 3, 2):
            xs = (x + s) % NX
            rcopy(
                fall.at[xs], fall.at[xs], f3_ssem.at[xs], f3_rsem.at[xs], sibling
            ).wait_recv()
            emit(xs)

    @pl.when(root)
    def _():
        @pl.loop(1, NZ)
        def _(s):
            rcopy(w_mine, w0_mine, az_ssem.at[s], az_rsem.at[0], sibling).wait_send()

        for s in range(4):
            for e in range(2):
                if s or e:
                    rcopy(
                        fall.at[x], fall.at[x], f2_ssem.at[s, e], f2_rsem.at[x], sibling
                    ).wait_send()

    @pl.loop(1, NF)
    def _(s):
        rcopy(dsend, drecv.at[f], d_ssem.at[s], d_rsem.at[f], sibling).wait_send()
        for n in range(2):
            rcopy(
                att_out.at[n, f], att_in.at[n, f], c_ssem.at[n, s], c_rsem.at[n, f], sibling
            ).wait_send()
            rcopy(
                g_out.at[n, f], g_in.at[n, f], g_ssem.at[n, s], g_rsem.at[n, f], sibling
            ).wait_send()

    for s in range(1, 4):
        for j, w in enumerate((w0_mine, w1_mine)):
            rcopy(w, w, a1_ssem.at[j, s], a1_rsem.at[j, 0], sibling).wait_send()
        for k in range(4):
            for j in range(2):
                rcopy(
                    w0_mine, w0_mine, a2_ssem.at[j, s, k], a2_rsem.at[j, 0, 0], sibling
                ).wait_send()
                to = ((x if j == 0 else y) + s) % 4
                rcopy(
                    w0_mine, w0_mine, b2_ssem.at[j, to, k], b2_rsem.at[j, 0, 0], sibling
                ).wait_send()
        for j, w in enumerate((t0.at[y], t1.at[x])):
            rcopy(w, w, b1_ssem.at[j, s], b1_rsem.at[j, 0], sibling).wait_send()
    att_copy.wait_send()
    c_copy.wait_send()
    g_copy.wait_send()
    for j in range(2):

        @pl.when(z != 4 * c + 2 * j + h)
        def _(j=j):
            rcopy(vb.at[j], zr.at[z], bz_ssem.at[j], bz_rsem.at[z], sibling).wait_send()

    @pl.when(active)
    def _():
        for s in range(4):
            rcopy(fall.at[s], fall.at[s], f3_ssem.at[s], f3_rsem.at[s], sibling).wait_send()

    for out in outs:
        out.wait()
    for i in range(4):
        pltpu.make_async_copy(
            fall.at[i], wg_hbm.at[:, QD * i : QD * (i + 1)], wg_sem.at[i]
        ).wait()


def finish(dq_in, dk_in, dv_in, wg_in, dq_out, dk_out, dv_out, wg_out, grads, wg_b, wg_f, sems):
    pairs = ((dq_in, dq_out), (dk_in, dk_out), (dv_in, dv_out))
    reads = [pltpu.make_async_copy(pairs[i][0], grads.at[i], sems.at[i]) for i in range(3)]
    reads.append(pltpu.make_async_copy(wg_in, wg_b, sems.at[3]))
    writes = [pltpu.make_async_copy(grads.at[i], pairs[i][1], sems.at[i]) for i in range(3)]
    writes.append(pltpu.make_async_copy(wg_f, wg_out, sems.at[3]))
    for read in reads:
        read.start()
    for i in range(3):
        reads[i].wait()
        writes[i].start()
    reads[3].wait()
    wg_f[...] = wg_b[...].astype(F32)
    for write in writes[3:]:
        write.start()
    for write in writes:
        write.wait()


def per_device(cotangent, out_weight, queries, key_vectors, value_vectors, destination, protein_ids):
    dma = pltpu.SemaphoreType.DMA
    vmem = pltpu.VMEM
    slots = jax.ShapeDtypeStruct((OWN, PAIRS * 128), BF16)
    any_space = pl.BlockSpec(memory_space=pl.ANY)
    in_vmem = pl.BlockSpec(memory_space=pltpu.VMEM)
    *grads, weight_grad = pl.pallas_call(
        kernel,
        out_shape=(slots, slots, slots, jax.ShapeDtypeStruct((ROWS, D), BF16)),
        in_specs=[any_space] * 5 + [in_vmem] * 2,
        out_specs=(any_space,) * 4,
        scratch_shapes=[
            *[vmem((OWN, PAIRS * 128), BF16) for _ in range(6)],
            vmem((8, TOK), jnp.int32),
            vmem((NF, 8, TOK), jnp.int32),
            vmem((2, TOK, D), BF16),
            vmem((NF * BLK, 5 * SPAD), BF16),
            vmem((NF * BLK, 5 * TOK), BF16),
            vmem((PAIRS, SPAD, 128), BF16),
            vmem((2, NF, BLK, 128), BF16),
            vmem((2, NF, BLK, 128), BF16),
            vmem((640, TOK), BF16),
            vmem((2, 640, TOK), BF16),
            vmem((PAIRS, 2 * OWN, OWN), F32),
            vmem((OWN, OWN), F32),
            vmem((NX, NY, ROWS, QD), BF16),
            vmem((NY, NX, ROWS, QD), BF16),
            vmem((2, 5, TOK, 128), BF16),
            vmem((5, TOK, 128), BF16),
            vmem((2, NF, BLK, 128), BF16),
            vmem((2, NF, BLK, 128), BF16),
            vmem((5, OWN, 128), BF16),
            *[vmem((4, 4, ROWS, QD), BF16) for _ in range(4)],
            *[vmem((4, ROWS, QD), BF16) for _ in range(4)],
            vmem((2, ROWS, QD), F32),
            vmem((2, ROWS, QD), BF16),
            vmem((NZ, ROWS, QD), BF16),
            vmem((NX, ROWS, QD), BF16),
            dma((4,)), dma((3,)), dma((4,)), dma,
            dma((NF,)), dma((NF,)), *[dma((2, NF)) for _ in range(4)],
            dma((NZ,)), dma((2,)), dma((2, 4)), dma((2, 4)), dma((2, 4, 4)), dma((2, 4, 4)),
            dma((3,)), dma((3,)),
            dma((2, 4, 4)), dma((2, 4, 4)), dma((2, 4)), dma((2, 4)), dma((2,)), dma((NZ,)),
            dma((4, 2)), dma((4,)), dma((4,)), dma((4,)),
        ],
        compiler_params=pltpu.CompilerParams(
            collective_id=0, has_side_effects=True, vmem_limit_bytes=56 * 1024 * 1024
        ),
    )(
        cotangent, out_weight, queries, key_vectors, value_vectors,
        destination.reshape(1, TOK), protein_ids.reshape(1, OWN),
    )
    return pl.pallas_call(
        finish,
        out_shape=(slots, slots, slots, jax.ShapeDtypeStruct((ROWS, D), F32)),
        in_specs=[any_space] * 4,
        out_specs=(any_space,) * 4,
        scratch_shapes=[vmem((3, OWN, PAIRS * 128), BF16), vmem((ROWS, D), BF16), vmem((ROWS, D), F32), dma((4,))],
    )(*grads, weight_grad)


def solution(mesh):
    rows = P(("dp", "fsdp"), None)
    return jax.shard_map(
        per_device,
        mesh=mesh,
        in_specs=(rows, P("fsdp", None), rows, rows, rows, P(("dp", "fsdp")), P(("dp", "fsdp"))),
        out_specs=(rows, rows, rows, P("fsdp", None)),
        check_vma=False,
    )
```

time: 110 us -> 102 us (0.927)
  the two profiles are of different devices: /device:TPU:49 before, /device:TPU:1 now
where the time goes in v2:
time: 102 us
  Pallas kernels  101 us (99%)
    pallas_call x1, Pallas kernels, per_device(): pl.pallas_call(kernel, out_shape=(slots, slots, slots, jax.ShapeDtypeStru...  98.5 us
    pallas_call x1, Pallas kernels, per_device(): pl.pallas_call(finish, out_shape=(slots, slots, slots, jax.ShapeDtypeStru...  2.44 us

profile of v2, /device:TPU:1, one launch (start us, length us, event | category | flops | bytes accessed | tf_op | source)
XLA Modules:
  0.0 101.6 jit_solution(3009075523598200911)
XLA Ops:
  0.6 98.5 %shard_map.102 = (bf16[192,1280]{1,0:T(8,128)(2,1)}, bf16[192,1280]{1,0:T(8,128)(2,1)}, bf16[192,1280]{1,0:T(8,128)(2,1)}, bf16[80,2560]{1,0:T(8,128)(2,1)}) custom-call(bf16[128,2560]{1,0:T(8,128)(2,1)} %cot_hbm.1, bf16[80,2560]{1,0:T(8,128)(2,1)} %w_hbm.1, bf16[192,1280]{1,0:T(8,128)(2,1)} %q_hbm.1, bf16[192,1280]{1,0:T(8,128)(2,1)} %k_hbm.1, ...), custom_call_target="tpu_custom_call" | custom-call | tf_op jit(solution)/shard_map/pallas_call | solution.py:589
  99.2 2.4 %shard_map.103 = (bf16[192,1280]{1,0:T(8,128)(2,1)}, bf16[192,1280]{1,0:T(8,128)(2,1)}, bf16[192,1280]{1,0:T(8,128)(2,1)}, f32[80,2560]{1,0:T(8,128)}) custom-call(bf16[192,1280]{1,0:T(8,128)(2,1)} %get-tuple-element.8.dq_in, bf16[192,1280]{1,0:T(8,128)(2,1)} %get-tuple-element.9.dk_in, bf16[192,1280]{1,0:T(8,128)(2,1)} %get-tuple-element.10.dv_in, ...), custom_call_target="tpu_custom_call" | custom-call | tf_op jit(solution)/shard_map/pallas_call | solution.py:635

commit v3 on v2

--- a/solution.py
+++ b/solution.py
@@ -53,12 +53,12 @@
     dsend, drecv, c_all, h_own, h_tok,
     att, att_out, att_in, att_t, att_all, probs, same_v,
     w0, w1, g_tmp, g_tok, g_out, g_in, g_v,
-    s0, s1, r0, r1, t0, t1, u0, u1, vf, vb, zr, fall,
+    s0, s1, r0, r1, m_in, m_out, t0, t1, u0, u1, vf, vb, zr, fall,
     load_sem, out_sem, wg_sem, own_sem,
     d_ssem, d_rsem, c_ssem, c_rsem, g_ssem, g_rsem,
     az_ssem, az_rsem, a1_ssem, a1_rsem, a2_ssem, a2_rsem,
     sib_ssem, sib_rsem,
-    b2_ssem, b2_rsem, b1_ssem, b1_rsem, bz_ssem, bz_rsem,
+    m_ssem, m_rsem, b2_ssem, b2_rsem, b1_ssem, b1_rsem, bz_ssem, bz_rsem,
     f2_ssem, f2_rsem, f3_ssem, f3_rsem,
 ):
     dp = lax.axis_index("dp")
@@ -230,12 +230,31 @@
 
     pl.loop(0, 2)(lambda i: forward(5 * c + i))
 
+    def lane(j):
+        if j == 0:
+            return w0, x, y, lambda at: dev(at, y, z, c)
+        return w1, y, x, lambda at: dev(x, at, z, c)
+
     def pass_on(j, k):
-        for s in (1, 3, 2):
-            ref = w0.at[x, k] if j == 0 else w1.at[y, k]
-            to = dev((x + s) % NX, y, z, c) if j == 0 else dev(x, (y + s) % NY, z, c)
-            me = x if j == 0 else y
-            rcopy(ref, ref, a2_ssem.at[j, s, k], a2_rsem.at[j, me, k], to).start()
+        ref, me, _, at = lane(j)
+        for s in (1, 3):
+            rcopy(
+                ref.at[me, k], ref.at[me, k], a2_ssem.at[j, s, k], a2_rsem.at[j, me, k],
+                at((me + s) % 4),
+            ).start()
+
+    def relay(e):
+        for j in range(2):
+            ref, me, first, at = lane(j)
+            k = (first + e) % 4
+            ahead_by = 1 if e % 2 == 0 else 3
+            behind = (me + 4 - ahead_by) % 4
+            block = ref.at[behind, k]
+            rcopy(block, block, a2_ssem.at[j, 2, k], a2_rsem.at[j, behind, k], sibling).wait_recv()
+            rcopy(
+                block, block, a2_ssem.at[j, 2, k], a2_rsem.at[j, behind, k],
+                at((me + ahead_by) % 4),
+            ).start()
 
     @pl.when(root)
     def _():
@@ -285,6 +304,8 @@
         rcopy(w1.at[y, xs], w1.at[y, xs], a1_ssem.at[1, s], a1_rsem.at[1, xs], sibling).wait_recv()
         pass_on(1, xs)
 
+    relay(0)
+
     def take_att(n):
         @pl.loop(1, NF)
         def _(s):
@@ -299,20 +320,47 @@
     att_t[...] = take_att(0)
     att_copy = rcopy(att_t, att_all.at[c], sib_ssem.at[0], sib_rsem.at[0], sibling)
     att_copy.start()
+    relay(1)
     att_all[c] = take_att(1)
+    relay(3)
     loads[3].wait()
     rcopy(cot_hbm, c_all.at[o], sib_ssem.at[1], sib_rsem.at[1], sibling).wait_recv()
     rcopy(att_t, att_all.at[o], sib_ssem.at[0], sib_rsem.at[0], sibling).wait_recv()
 
-    def share_out(j, to, k):
+    def sums_lane(j):
         if j == 0:
-            src, dst, me, device = s0.at[to, k], r0.at[x, k], x, dev(to, y, z, c)
-        else:
-            src, dst, me, device = s1.at[to, k], r1.at[y, k], y, dev(x, to, z, c)
-        rcopy(src, dst, b2_ssem.at[j, to, k], b2_rsem.at[j, me, k], device).start()
+            return s0, r0, x, y, lambda at: dev(at, y, z, c)
+        return s1, r1, y, x, lambda at: dev(x, at, z, c)
+
+    def far_out(j, e):
+        own, _, me, first, at = sums_lane(j)
+        k = (first + e) % 4
+        ahead_by = 1 if e % 2 == 0 else 3
+        rcopy(
+            own.at[(me + 2) % 4, k], m_in.at[j, k], m_ssem.at[j, k], m_rsem.at[j, k],
+            at((me + ahead_by) % 4),
+        ).start()
+
+    def near_out(j, e):
+        own, ins, me, first, at = sums_lane(j)
+        k = (first + e) % 4
+        behind = (me + (3 if e % 2 == 0 else 1)) % 4
+        rcopy(
+            own.at[behind, k], ins.at[me, k], b2_ssem.at[j, 0, k], b2_rsem.at[j, me, k], at(behind)
+        ).start()
+
+    def sum_out(j, e):
+        own, ins, me, first, at = sums_lane(j)
+        k = (first + e) % 4
+        to = (me + (1 if e % 2 == 0 else 3)) % 4
+        rcopy(m_in.at[j, k], m_in.at[j, k], m_ssem.at[j, k], m_rsem.at[j, k], sibling).wait_recv()
+        m_out[j, k] = (own[to, k].astype(F32) + m_in[j, k].astype(F32)).astype(BF16)
+        rcopy(
+            m_out.at[j, k], ins.at[me, k], b2_ssem.at[j, 1, k], b2_rsem.at[j, me, k], at(to)
+        ).start()
 
     att_both = jnp.concatenate([att_all[0], att_all[1]], axis=1)
-    for s in (1, 2, 3, 0):
+    for s in (2, 1, 3, 0):
         xs = (x + s) % NX
         cols = c_all[:, :, pl.ds(pl.multiple_of(xs * QD, 128), QD)].reshape(2 * TOK, QD)
         share = dot_nn(att_both, cols)
@@ -321,19 +369,28 @@
             s0[xs, ys] = share[ROWS * n : ROWS * (n + 1)].astype(BF16)
             n = row_of(ys, 1)
             s1[ys, xs] = share[ROWS * n : ROWS * (n + 1)].astype(BF16)
-        if s:
-            share_out(0, xs, (y + 1) % NY)
-        for e in (1, 3, 2):
-            share_out(1, (y + e) % NY, xs)
-    for e in (2, 3, 0):
-        for s in (1, 3, 2):
-            share_out(0, (x + s) % NX, (y + e) % NY)
-
-    for s in range(1, 4):
-        xs, ys = (x + s) % NX, (y + s) % NY
-        for k in range(4):
-            for j, ref, frm in ((0, w0.at[xs, k], xs), (1, w1.at[ys, k], ys)):
-                rcopy(ref, ref, a2_ssem.at[j, s, k], a2_rsem.at[j, frm, k], sibling).wait_recv()
+        far_out(1, s)
+        if s == 2:
+            for e in (2, 1, 3, 0):
+                far_out(0, e)
+        if s % 2:
+            for e in (2, 0) if s == 3 else (1, 3):
+                near_out(0, e)
+        near_out(1, s)
+    relay(2)
+    for e in (2, 1, 3, 0):
+        for j in range(2):
+            sum_out(j, e)
+
+    for e in range(4):
+        for j in range(2):
+            ref, me, first, _ = lane(j)
+            k = (first + e) % 4
+            for s in (1 if e % 2 == 0 else 3, 2):
+                block = ref.at[(me + s) % 4, k]
+                rcopy(
+                    block, block, a2_ssem.at[j, s, k], a2_rsem.at[j, (me + s) % 4, k], sibling
+                ).wait_recv()
     total = None
     for k in range(4):
         blocks = []
@@ -367,7 +424,7 @@
     rcopy(g_tmp.at[o], g_tok, sib_ssem.at[2], sib_rsem.at[2], sibling).wait_recv()
     send_grad(1, g_tok[...])
 
-    for e in (1, 2, 3, 0):
+    for e in (2, 1, 3, 0):
         for j in range(2):
             if j == 0:
                 own, ins, out, nxt, me, k = s0, r0, t0, u0, x, (y + e) % NY
@@ -376,7 +433,7 @@
                 own, ins, out, nxt, me, k = s1, r1, t1, u1, y, (x + e) % NX
                 after, to = x, dev(k, y, z, c)
             acc = own[me, k].astype(F32)
-            for s in (1, 3, 2):
+            for s in (1, 3):
                 frm = (me + s) % 4
                 rcopy(
                     own.at[frm, k], ins.at[frm, k], b2_ssem.at[j, 0, 0], b2_rsem.at[j, frm, k],
@@ -533,12 +590,14 @@
                 rcopy(
                     w0_mine, w0_mine, a2_ssem.at[j, s, k], a2_rsem.at[j, 0, 0], sibling
                 ).wait_send()
-                to = ((x if j == 0 else y) + s) % 4
-                rcopy(
-                    w0_mine, w0_mine, b2_ssem.at[j, to, k], b2_rsem.at[j, 0, 0], sibling
-                ).wait_send()
         for j, w in enumerate((t0.at[y], t1.at[x])):
             rcopy(w, w, b1_ssem.at[j, s], b1_rsem.at[j, 0], sibling).wait_send()
+    for j in range(2):
+        for k in range(4):
+            block = m_in.at[j, k]
+            rcopy(block, block, m_ssem.at[j, k], m_rsem.at[j, k], sibling).wait_send()
+            for s in range(2):
+                rcopy(block, block, b2_ssem.at[j, s, k], m_rsem.at[j, k], sibling).wait_send()
     att_copy.wait_send()
     c_copy.wait_send()
     g_copy.wait_send()
@@ -613,6 +672,7 @@
             vmem((2, NF, BLK, 128), BF16),
             vmem((5, OWN, 128), BF16),
             *[vmem((4, 4, ROWS, QD), BF16) for _ in range(4)],
+            *[vmem((2, 4, ROWS, QD), BF16) for _ in range(2)],
             *[vmem((4, ROWS, QD), BF16) for _ in range(4)],
             vmem((2, ROWS, QD), F32),
             vmem((2, ROWS, QD), BF16),
@@ -622,7 +682,8 @@
             dma((NF,)), dma((NF,)), *[dma((2, NF)) for _ in range(4)],
             dma((NZ,)), dma((2,)), dma((2, 4)), dma((2, 4)), dma((2, 4, 4)), dma((2, 4, 4)),
             dma((3,)), dma((3,)),
-            dma((2, 4, 4)), dma((2, 4, 4)), dma((2, 4)), dma((2, 4)), dma((2,)), dma((NZ,)),
+            dma((2, 4)), dma((2, 4)), dma((2, 2, 4)), dma((2, 4, 4)),
+            dma((2, 4)), dma((2, 4)), dma((2,)), dma((NZ,)),
             dma((4, 2)), dma((4,)), dma((4,)), dma((4,)),
         ],
         compiler_params=pltpu.CompilerParams(

time: 102 us -> 92.5 us (0.907)
  Pallas kernels: 101 us -> 91.8 us
    pallas_call x1, Pallas kernels: 98.5 us -> 89.3 us  [per_device(): pl.pallas_call(kernel, out_shape=(slots, slots, slots, jax.ShapeDtypeStru...]
where the time goes in v3:
time: 92.5 us; the launch traced here: 92.4 us
  Pallas kernels  91.8 us (99%)
    pallas_call x1, Pallas kernels, per_device(): pl.pallas_call(kernel, out_shape=(slots, slots, slots, jax.ShapeDtypeStru...  89.3 us
    pallas_call x1, Pallas kernels, per_device(): pl.pallas_call(finish, out_shape=(slots, slots, slots, jax.ShapeDtypeStru...  2.44 us

profile of v3, /device:TPU:1, one launch (start us, length us, event | category | flops | bytes accessed | tf_op | source)
XLA Modules:
  0.0 92.4 jit_solution(18056014338500625549)
XLA Ops:
  0.6 89.3 %shard_map.102 = (bf16[192,1280]{1,0:T(8,128)(2,1)}, bf16[192,1280]{1,0:T(8,128)(2,1)}, bf16[192,1280]{1,0:T(8,128)(2,1)}, bf16[80,2560]{1,0:T(8,128)(2,1)}) custom-call(bf16[128,2560]{1,0:T(8,128)(2,1)} %cot_hbm.1, bf16[80,2560]{1,0:T(8,128)(2,1)} %w_hbm.1, bf16[192,1280]{1,0:T(8,128)(2,1)} %q_hbm.1, bf16[192,1280]{1,0:T(8,128)(2,1)} %k_hbm.1, ...), custom_call_target="tpu_custom_call" | custom-call | tf_op jit(solution)/shard_map/pallas_call | solution.py:648
  90.0 2.4 %shard_map.103 = (bf16[192,1280]{1,0:T(8,128)(2,1)}, bf16[192,1280]{1,0:T(8,128)(2,1)}, bf16[192,1280]{1,0:T(8,128)(2,1)}, f32[80,2560]{1,0:T(8,128)}) custom-call(bf16[192,1280]{1,0:T(8,128)(2,1)} %get-tuple-element.8.dq_in, bf16[192,1280]{1,0:T(8,128)(2,1)} %get-tuple-element.9.dk_in, bf16[192,1280]{1,0:T(8,128)(2,1)} %get-tuple-element.10.dv_in, ...), custom_call_target="tpu_custom_call" | custom-call | tf_op jit(solution)/shard_map/pallas_call | solution.py:696

commit v4 on v3

--- a/solution.py
+++ b/solution.py
@@ -16,6 +16,8 @@
 D = 2560
 QD = D // 4
 ROWS = 80
+GATHER = ((0, 32), (32, 48))
+SPREAD = ((0, 48), (48, 32))
 BLK = 64
 SPAD = 256
 PAIRS = 10
@@ -127,42 +129,6 @@
     )
     first_head = lax.broadcasted_iota(jnp.int32, (OWN, 128), 1) < 64
 
-    pl.semaphore_wait(barrier, 25)
-
-    @pl.loop(1, NF)
-    def _(s):
-        rcopy(dsend, drecv.at[f], d_ssem.at[s], d_rsem.at[f], (dp, (f + s) % NF)).start()
-
-    drecv[f] = dsend[...]
-
-    active = z // 4 == c
-    root = jnp.logical_and(active, z % 2 == h)
-    root_j = (z % 4) // 2
-    w_mine = w_hbm.at[:, pl.ds(pl.multiple_of(x * QD, 128), QD)]
-
-    def spread_z(dst):
-        pltpu.make_async_copy(w_mine, dst, own_sem).start()
-
-        @pl.loop(1, NZ)
-        def _(s):
-            rcopy(
-                w_mine, dst, az_ssem.at[s], az_rsem.at[root_j], dev(x, y, (z + s) % NZ, c)
-            ).start()
-
-    w0_mine = w0.at[x, y]
-    w1_mine = w1.at[y, x]
-
-    @pl.when(jnp.logical_and(root, root_j == 0))
-    def _():
-        spread_z(w0_mine)
-
-    @pl.when(jnp.logical_and(root, root_j == 1))
-    def _():
-        spread_z(w1_mine)
-
-    c_copy = rcopy(cot_hbm, c_all.at[c], sib_ssem.at[1], sib_rsem.at[1], sibling)
-    c_copy.start()
-
     def both_heads(rows):
         return jnp.concatenate([rows * head_masks[0], rows * head_masks[1]], axis=0)
 
@@ -181,7 +147,46 @@
 
     for load in loads[:3]:
         load.wait()
-    pl.loop(0, 5)(lambda i: forward(5 * o + i))
+    pl.loop(0, 2)(lambda i: forward(5 * o + i))
+    pl.semaphore_wait(barrier, 25)
+
+    @pl.loop(1, NF)
+    def _(s):
+        rcopy(dsend, drecv.at[f], d_ssem.at[s], d_rsem.at[f], (dp, (f + s) % NF)).start()
+
+    drecv[f] = dsend[...]
+
+    active = z // 4 == c
+    root = jnp.logical_and(active, z % 2 == h)
+    root_j = (z % 4) // 2
+    w_mine = w_hbm.at[:, pl.ds(pl.multiple_of(x * QD, 128), QD)]
+
+    def spread_z(dst):
+        for q, rows in enumerate(GATHER):
+            src, to = w_mine.at[pl.ds(*rows)], dst.at[pl.ds(*rows)]
+            pltpu.make_async_copy(src, to, own_sem.at[q]).start()
+
+            @pl.loop(1, NZ)
+            def _(s, q=q, src=src, to=to):
+                rcopy(
+                    src, to, az_ssem.at[s, q], az_rsem.at[root_j, q], dev(x, y, (z + s) % NZ, c)
+                ).start()
+
+    w0_mine = w0.at[x, y]
+    w1_mine = w1.at[y, x]
+
+    @pl.when(jnp.logical_and(root, root_j == 0))
+    def _():
+        spread_z(w0_mine)
+
+    @pl.when(jnp.logical_and(root, root_j == 1))
+    def _():
+        spread_z(w1_mine)
+
+    c_copy = rcopy(cot_hbm, c_all.at[c], sib_ssem.at[1], sib_rsem.at[1], sibling)
+    c_copy.start()
+
+    pl.loop(2, 5)(lambda i: forward(5 * o + i))
 
     @pl.loop(1, NF)
     def _(s):
@@ -228,58 +233,55 @@
 
     send_att(0, o)
 
-    pl.loop(0, 2)(lambda i: forward(5 * c + i))
 
     def lane(j):
         if j == 0:
             return w0, x, y, lambda at: dev(at, y, z, c)
         return w1, y, x, lambda at: dev(x, at, z, c)
 
-    def pass_on(j, k):
+    def pass_on(j, k, q):
         ref, me, _, at = lane(j)
+        piece = ref.at[me, k, pl.ds(*GATHER[q])]
         for s in (1, 3):
             rcopy(
-                ref.at[me, k], ref.at[me, k], a2_ssem.at[j, s, k], a2_rsem.at[j, me, k],
-                at((me + s) % 4),
+                piece, piece, a2_ssem.at[j, s, k, q], a2_rsem.at[j, me, k, q], at((me + s) % 4)
             ).start()
 
     def relay(e):
-        for j in range(2):
-            ref, me, first, at = lane(j)
-            k = (first + e) % 4
-            ahead_by = 1 if e % 2 == 0 else 3
-            behind = (me + 4 - ahead_by) % 4
-            block = ref.at[behind, k]
-            rcopy(block, block, a2_ssem.at[j, 2, k], a2_rsem.at[j, behind, k], sibling).wait_recv()
-            rcopy(
-                block, block, a2_ssem.at[j, 2, k], a2_rsem.at[j, behind, k],
-                at((me + ahead_by) % 4),
-            ).start()
-
-    @pl.when(root)
-    def _():
-        pltpu.make_async_copy(w_mine, w0_mine, own_sem).wait()
-
-    @pl.when(z != 4 * c + h)
-    def _():
-        rcopy(w0_mine, w0_mine, az_ssem.at[0], az_rsem.at[0], sibling).wait_recv()
-
-    for s in (1, 3, 2):
-        rcopy(
-            w0_mine, w0_mine, a1_ssem.at[0, s], a1_rsem.at[0, y], dev(x, (y + s) % NY, z, c)
-        ).start()
-    pass_on(0, y)
-
-    @pl.when(z != 4 * c + 2 + h)
-    def _():
-        rcopy(w1_mine, w1_mine, az_ssem.at[0], az_rsem.at[1], sibling).wait_recv()
-
-    for s in (1, 3, 2):
-        rcopy(
-            w1_mine, w1_mine, a1_ssem.at[1, s], a1_rsem.at[1, x], dev((x + s) % NX, y, z, c)
-        ).start()
-    pass_on(1, x)
-
+        for q, rows in enumerate(GATHER):
+            for j in range(2):
+                ref, me, first, at = lane(j)
+                k = (first + e) % 4
+                ahead_by = 1 if e % 2 == 0 else 3
+                behind = (me + 4 - ahead_by) % 4
+                piece = ref.at[behind, k, pl.ds(*rows)]
+                sems = a2_ssem.at[j, 2, k, q], a2_rsem.at[j, behind, k, q]
+                rcopy(piece, piece, *sems, sibling).wait_recv()
+                rcopy(piece, piece, *sems, at((me + ahead_by) % 4)).start()
+
+    def begin(q):
+        rows = pl.ds(*GATHER[q])
+
+        @pl.when(root)
+        def _():
+            pltpu.make_async_copy(w_mine.at[rows], w0_mine.at[rows], own_sem.at[q]).wait()
+
+        for j, mine in enumerate((w0_mine, w1_mine)):
+            piece = mine.at[rows]
+
+            @pl.when(z != 4 * c + 2 * j + h)
+            def _(j=j, piece=piece):
+                rcopy(piece, piece, az_ssem.at[0, q], az_rsem.at[j, q], sibling).wait_recv()
+
+            me = y if j == 0 else x
+            for s in (1, 3, 2):
+                to = dev(x, (y + s) % NY, z, c) if j == 0 else dev((x + s) % NX, y, z, c)
+                rcopy(piece, piece, a1_ssem.at[j, s, q], a1_rsem.at[j, me, q], to).start()
+            pass_on(j, me, q)
+
+    begin(0)
+    pl.loop(0, 2)(lambda i: forward(5 * c + i))
+    begin(1)
     pl.loop(2, 5)(lambda i: forward(5 * c + i))
     send_att(1, c)
 
@@ -299,10 +301,11 @@
 
     for s in (1, 3, 2):
         ys, xs = (y + s) % NY, (x + s) % NX
-        rcopy(w0.at[x, ys], w0.at[x, ys], a1_ssem.at[0, s], a1_rsem.at[0, ys], sibling).wait_recv()
-        pass_on(0, ys)
-        rcopy(w1.at[y, xs], w1.at[y, xs], a1_ssem.at[1, s], a1_rsem.at[1, xs], sibling).wait_recv()
-        pass_on(1, xs)
+        for q, rows in enumerate(GATHER):
+            for j, ref, k in ((0, w0.at[x, ys], ys), (1, w1.at[y, xs], xs)):
+                piece = ref.at[pl.ds(*rows)]
+                rcopy(piece, piece, a1_ssem.at[j, s, q], a1_rsem.at[j, k, q], sibling).wait_recv()
+                pass_on(j, k, q)
 
     relay(0)
 
@@ -387,10 +390,12 @@
             ref, me, first, _ = lane(j)
             k = (first + e) % 4
             for s in (1 if e % 2 == 0 else 3, 2):
-                block = ref.at[(me + s) % 4, k]
-                rcopy(
-                    block, block, a2_ssem.at[j, s, k], a2_rsem.at[j, (me + s) % 4, k], sibling
-                ).wait_recv()
+                for q, rows in enumerate(GATHER):
+                    piece = ref.at[(me + s) % 4, k, pl.ds(*rows)]
+                    rcopy(
+                        piece, piece, a2_ssem.at[j, s, k, q], a2_rsem.at[j, (me + s) % 4, k, q],
+                        sibling,
+                    ).wait_recv()
     total = None
     for k in range(4):
         blocks = []
@@ -462,9 +467,11 @@
 
         @pl.when(z != z_root)
         def _(j=j, z_root=z_root):
-            rcopy(
-                vb.at[j], zr.at[z], bz_ssem.at[j], bz_rsem.at[z], dev(x, y, z_root, c)
-            ).start()
+            for q, rows in enumerate(SPREAD):
+                rcopy(
+                    vb.at[j, pl.ds(*rows)], zr.at[z, pl.ds(*rows)], bz_ssem.at[j, q],
+                    bz_rsem.at[z, q], dev(x, y, z_root, c),
+                ).start()
 
     def take_grad(n):
         @pl.loop(1, NF)
@@ -501,7 +508,45 @@
     take_grad(0)
     pl.loop(0, 5)(lambda i: backward(5 * c + i, g_v[i]))
     take_grad(1)
-    pl.loop(0, 5)(lambda i: backward(5 * o + i, g_v[i]))
+    pl.loop(0, 2)(lambda i: backward(5 * o + i, g_v[i]))
+    def piece_of(i, q):
+        return fall.at[i, pl.ds(*SPREAD[q])]
+
+    def emit(i, q):
+        pltpu.make_async_copy(
+            piece_of(i, q),
+            wg_hbm.at[pl.ds(*SPREAD[q]), pl.ds(pl.multiple_of(i * QD, 128), QD)],
+            wg_sem.at[i, q],
+        ).start()
+
+    def to_sibling(i, q):
+        piece = piece_of(i, q)
+        rcopy(piece, piece, f3_ssem.at[i, q], f3_rsem.at[i, q], sibling).start()
+        emit(i, q)
+
+    @pl.when(root)
+    def _():
+        for q, (top, count) in enumerate(SPREAD):
+            acc = vf[root_j, top : top + count]
+            for s in range(1, NZ):
+                frm = (z + s) % NZ
+                rows = pl.ds(top, count)
+                rcopy(
+                    vb.at[0, rows], zr.at[frm, rows], bz_ssem.at[0, q], bz_rsem.at[frm, q], sibling
+                ).wait_recv()
+                acc += zr[frm, top : top + count].astype(F32)
+            fall[x, top : top + count] = acc.astype(BF16)
+            piece = piece_of(x, q)
+            for s in (1, 3, 2, 0):
+                for e in (2, 0):
+                    if s or e:
+                        rcopy(
+                            piece, piece, f2_ssem.at[s, e // 2, q], f2_rsem.at[x, q],
+                            dev((x + s) % NX, (y + e) % NY, z, c),
+                        ).start()
+            to_sibling(x, q)
+
+    pl.loop(2, 5)(lambda i: backward(5 * o + i, g_v[i]))
     outs = [
         pltpu.make_async_copy(src, dst, out_sem.at[i])
         for i, (src, dst) in enumerate(((dq_v, dq_hbm), (dk_v, dk_hbm), (dv_v, dv_hbm)))
@@ -509,67 +554,46 @@
     for out in outs:
         out.start()
 
-    def emit(i):
-        pltpu.make_async_copy(
-            fall.at[i],
-            wg_hbm.at[:, pl.ds(pl.multiple_of(i * QD, 128), QD)],
-            wg_sem.at[i],
-        ).start()
-
-    def to_sibling(i):
-        rcopy(fall.at[i], fall.at[i], f3_ssem.at[i], f3_rsem.at[i], sibling).start()
-        emit(i)
-
-    @pl.when(root)
-    def _():
-        acc = vf[root_j]
-        for s in range(1, NZ):
-            frm = (z + s) % NZ
-            rcopy(vb.at[0], zr.at[frm], bz_ssem.at[0], bz_rsem.at[frm], sibling).wait_recv()
-            acc += zr[frm].astype(F32)
-        fall[x] = acc.astype(BF16)
-        for s in (1, 3, 2, 0):
-            for e in (2, 0):
-                if s or e:
-                    rcopy(
-                        fall.at[x], fall.at[x], f2_ssem.at[s, e // 2], f2_rsem.at[x],
-                        dev((x + s) % NX, (y + e) % NY, z, c),
-                    ).start()
-        to_sibling(x)
-
-    @pl.when(jnp.logical_and(active, z % 2 != h))
-    def _():
-        rcopy(fall.at[x], fall.at[x], f2_ssem.at[0, 0], f2_rsem.at[x], sibling).wait_recv()
-        to_sibling(x)
-
-    @pl.when(active)
-    def _():
-        for s in (1, 3, 2):
-            xs = (x + s) % NX
-            rcopy(fall.at[xs], fall.at[xs], f2_ssem.at[0, 0], f2_rsem.at[xs], sibling).wait_recv()
-            to_sibling(xs)
-
-    @pl.when(jnp.logical_not(active))
-    def _():
-        for s in (0, 1, 3, 2):
-            xs = (x + s) % NX
-            rcopy(
-                fall.at[xs], fall.at[xs], f3_ssem.at[xs], f3_rsem.at[xs], sibling
-            ).wait_recv()
-            emit(xs)
+    for q in range(2):
+
+        @pl.when(jnp.logical_and(active, z % 2 != h))
+        def _(q=q):
+            piece = piece_of(x, q)
+            rcopy(piece, piece, f2_ssem.at[0, 0, q], f2_rsem.at[x, q], sibling).wait_recv()
+            to_sibling(x, q)
+
+        @pl.when(active)
+        def _(q=q):
+            for s in (1, 3, 2):
+                xs = (x + s) % NX
+                piece = piece_of(xs, q)
+                rcopy(piece, piece, f2_ssem.at[0, 0, q], f2_rsem.at[xs, q], sibling).wait_recv()
+                to_sibling(xs, q)
+
+        @pl.when(jnp.logical_not(active))
+        def _(q=q):
+            for s in (0, 1, 3, 2):
+                xs = (x + s) % NX
+                piece = piece_of(xs, q)
+                rcopy(piece, piece, f3_ssem.at[xs, q], f3_rsem.at[xs, q], sibling).wait_recv()
+                emit(xs, q)
 
     @pl.when(root)
     def _():
         @pl.loop(1, NZ)
         def _(s):
-            rcopy(w_mine, w0_mine, az_ssem.at[s], az_rsem.at[0], sibling).wait_send()
-
-        for s in range(4):
-            for e in range(2):
-                if s or e:
-                    rcopy(
-                        fall.at[x], fall.at[x], f2_ssem.at[s, e], f2_rsem.at[x], sibling
-                    ).wait_send()
+            for q, rows in enumerate(GATHER):
+                src, dst = w_mine.at[pl.ds(*rows)], w0_mine.at[pl.ds(*rows)]
+                rcopy(src, dst, az_ssem.at[s, q], az_rsem.at[0, q], sibling).wait_send()
+
+        for q in range(2):
+            piece = piece_of(x, q)
+            for s in range(4):
+                for e in range(2):
+                    if s or e:
+                        rcopy(
+                            piece, piece, f2_ssem.at[s, e, q], f2_rsem.at[x, q], sibling
+                        ).wait_send()
 
     @pl.loop(1, NF)
     def _(s):
@@ -583,13 +607,14 @@
             ).wait_send()
 
     for s in range(1, 4):
-        for j, w in enumerate((w0_mine, w1_mine)):
-            rcopy(w, w, a1_ssem.at[j, s], a1_rsem.at[j, 0], sibling).wait_send()
-        for k in range(4):
+        for q, rows in enumerate(GATHER):
+            piece = w0_mine.at[pl.ds(*rows)]
             for j in range(2):
-                rcopy(
-                    w0_mine, w0_mine, a2_ssem.at[j, s, k], a2_rsem.at[j, 0, 0], sibling
-                ).wait_send()
+                rcopy(piece, piece, a1_ssem.at[j, s, q], a1_rsem.at[j, 0, q], sibling).wait_send()
+                for k in range(4):
+                    rcopy(
+                        piece, piece, a2_ssem.at[j, s, k, q], a2_rsem.at[j, 0, 0, q], sibling
+                    ).wait_send()
         for j, w in enumerate((t0.at[y], t1.at[x])):
             rcopy(w, w, b1_ssem.at[j, s], b1_rsem.at[j, 0], sibling).wait_send()
     for j in range(2):
@@ -605,19 +630,28 @@
 
         @pl.when(z != 4 * c + 2 * j + h)
         def _(j=j):
-            rcopy(vb.at[j], zr.at[z], bz_ssem.at[j], bz_rsem.at[z], sibling).wait_send()
+            for q, rows in enumerate(SPREAD):
+                rows = pl.ds(*rows)
+                rcopy(
+                    vb.at[j, rows], zr.at[z, rows], bz_ssem.at[j, q], bz_rsem.at[z, q], sibling
+                ).wait_send()
 
     @pl.when(active)
     def _():
         for s in range(4):
-            rcopy(fall.at[s], fall.at[s], f3_ssem.at[s], f3_rsem.at[s], sibling).wait_send()
+            for q in range(2):
+                piece = piece_of(s, q)
+                rcopy(piece, piece, f3_ssem.at[s, q], f3_rsem.at[s, q], sibling).wait_send()
 
     for out in outs:
         out.wait()
     for i in range(4):
-        pltpu.make_async_copy(
-            fall.at[i], wg_hbm.at[:, QD * i : QD * (i + 1)], wg_sem.at[i]
-        ).wait()
+        for q, rows in enumerate(SPREAD):
+            pltpu.make_async_copy(
+                piece_of(i, q),
+                wg_hbm.at[pl.ds(*rows), QD * i : QD * (i + 1)],
+                wg_sem.at[i, q],
+            ).wait()
 
 
 def finish(dq_in, dk_in, dv_in, wg_in, dq_out, dk_out, dv_out, wg_out, grads, wg_b, wg_f, sems):
@@ -678,13 +712,14 @@
             vmem((2, ROWS, QD), BF16),
             vmem((NZ, ROWS, QD), BF16),
             vmem((NX, ROWS, QD), BF16),
-            dma((4,)), dma((3,)), dma((4,)), dma,
+            dma((4,)), dma((3,)), dma((4, 2)), dma((2,)),
             dma((NF,)), dma((NF,)), *[dma((2, NF)) for _ in range(4)],
-            dma((NZ,)), dma((2,)), dma((2, 4)), dma((2, 4)), dma((2, 4, 4)), dma((2, 4, 4)),
+            dma((NZ, 2)), dma((2, 2)), dma((2, 4, 2)), dma((2, 4, 2)),
+            dma((2, 4, 4, 2)), dma((2, 4, 4, 2)),
             dma((3,)), dma((3,)),
             dma((2, 4)), dma((2, 4)), dma((2, 2, 4)), dma((2, 4, 4)),
-            dma((2, 4)), dma((2, 4)), dma((2,)), dma((NZ,)),
-            dma((4, 2)), dma((4,)), dma((4,)), dma((4,)),
+            dma((2, 4)), dma((2, 4)), dma((2, 2)), dma((NZ, 2)),
+            dma((4, 2, 2)), dma((4, 2)), dma((4, 2)), dma((4, 2)),
         ],
         compiler_params=pltpu.CompilerParams(
             collective_id=0, has_side_effects=True, vmem_limit_bytes=56 * 1024 * 1024

time: 92.5 us -> 91.9 us (level); the launches traced: 92.4 us -> 90.8 us
  Pallas kernels: 91.8 us -> 90.1 us
    pallas_call x1, Pallas kernels: 89.3 us -> 87.7 us  [per_device(): pl.pallas_call(kernel, out_shape=(slots, slots, slots, jax.ShapeDtypeStru...]
where the time goes in v4:
time: 91.9 us; the launch traced here: 90.8 us
  Pallas kernels  90.1 us (98%)
    pallas_call x1, Pallas kernels, per_device(): pl.pallas_call(kernel, out_shape=(slots, slots, slots, jax.ShapeDtypeStru...  87.7 us
    pallas_call x1, Pallas kernels, per_device(): pl.pallas_call(finish, out_shape=(slots, slots, slots, jax.ShapeDtypeStru...  2.44 us

profile of v4, /device:TPU:1, one launch (start us, length us, event | category | flops | bytes accessed | tf_op | source)
XLA Modules:
  0.0 90.8 jit_solution(17879401125970243225)
XLA Ops:
  0.6 87.7 %shard_map.102 = (bf16[192,1280]{1,0:T(8,128)(2,1)}, bf16[192,1280]{1,0:T(8,128)(2,1)}, bf16[192,1280]{1,0:T(8,128)(2,1)}, bf16[80,2560]{1,0:T(8,128)(2,1)}) custom-call(bf16[128,2560]{1,0:T(8,128)(2,1)} %cot_hbm.1, bf16[80,2560]{1,0:T(8,128)(2,1)} %w_hbm.1, bf16[192,1280]{1,0:T(8,128)(2,1)} %q_hbm.1, bf16[192,1280]{1,0:T(8,128)(2,1)} %k_hbm.1, ...), custom_call_target="tpu_custom_call" | custom-call | tf_op jit(solution)/shard_map/pallas_call | solution.py:682
  88.3 2.4 %shard_map.103 = (bf16[192,1280]{1,0:T(8,128)(2,1)}, bf16[192,1280]{1,0:T(8,128)(2,1)}, bf16[192,1280]{1,0:T(8,128)(2,1)}, f32[80,2560]{1,0:T(8,128)}) custom-call(bf16[192,1280]{1,0:T(8,128)(2,1)} %get-tuple-element.8.dq_in, bf16[192,1280]{1,0:T(8,128)(2,1)} %get-tuple-element.9.dk_in, bf16[192,1280]{1,0:T(8,128)(2,1)} %get-tuple-element.10.dv_in, ...), custom_call_target="tpu_custom_call" | custom-call | tf_op jit(solution)/shard_map/pallas_call | solution.py:731

commit v5 on v4

--- a/solution.py
+++ b/solution.py
@@ -132,22 +132,24 @@
     def both_heads(rows):
         return jnp.concatenate([rows * head_masks[0], rows * head_masks[1]], axis=0)
 
-    def forward(p):
-        at = pl.ds(pl.multiple_of(p * 128, 128), 128)
-        qp, kp, vp = q_v[:, at], k_v[:, at], v_v[:, at]
-        scores = dot_nt(both_heads(qp), kp) * SCALE
-        same = jnp.concatenate([same_v[...], same_v[...]], axis=0)
-        scores = jnp.where(same > 0.0, scores, -1e30)
-        top = jnp.max(scores, axis=1, keepdims=True)
-        e = jnp.exp(scores - top)
-        prob = e * (1.0 / jnp.sum(e, axis=1, keepdims=True))
-        probs[p] = prob
-        out = dot_nn(prob.astype(BF16), vp)
-        att[p, 0:OWN] = jnp.where(first_head, out[:OWN], out[OWN:]).astype(BF16)
+    def forward(pairs):
+        at = [pl.ds(pl.multiple_of(p * 128, 128), 128) for p in pairs]
+        same = jnp.concatenate([same_v[...], same_v[...]], axis=0) > 0.0
+        values = [v_v[:, a] for a in at]
+        scores = [dot_nt(both_heads(q_v[:, a]), k_v[:, a]) * SCALE for a in at]
+        scores = [jnp.where(same, t, -1e30) for t in scores]
+        tops = [jnp.max(t, axis=1, keepdims=True) for t in scores]
+        exps = [jnp.exp(t - top) for t, top in zip(scores, tops)]
+        sums = [jnp.sum(e, axis=1, keepdims=True) for e in exps]
+        prob = [e * (1.0 / t) for e, t in zip(exps, sums)]
+        outs = [dot_nn(t.astype(BF16), v) for t, v in zip(prob, values)]
+        for p, t, out in zip(pairs, prob, outs):
+            probs[p] = t
+            att[p, 0:OWN] = jnp.where(first_head, out[:OWN], out[OWN:]).astype(BF16)
 
     for load in loads[:3]:
         load.wait()
-    pl.loop(0, 2)(lambda i: forward(5 * o + i))
+    forward([5 * o + i for i in range(2)])
     pl.semaphore_wait(barrier, 25)
 
     @pl.loop(1, NF)
@@ -186,7 +188,7 @@
     c_copy = rcopy(cot_hbm, c_all.at[c], sib_ssem.at[1], sib_rsem.at[1], sibling)
     c_copy.start()
 
-    pl.loop(2, 5)(lambda i: forward(5 * o + i))
+    forward([5 * o + i for i in range(2, 5)])
 
     @pl.loop(1, NF)
     def _(s):
@@ -274,15 +276,15 @@
                 rcopy(piece, piece, az_ssem.at[0, q], az_rsem.at[j, q], sibling).wait_recv()
 
             me = y if j == 0 else x
-            for s in (1, 3, 2):
+            for s in (1, 3):
                 to = dev(x, (y + s) % NY, z, c) if j == 0 else dev((x + s) % NX, y, z, c)
                 rcopy(piece, piece, a1_ssem.at[j, s, q], a1_rsem.at[j, me, q], to).start()
             pass_on(j, me, q)
 
     begin(0)
-    pl.loop(0, 2)(lambda i: forward(5 * c + i))
+    forward([5 * c + i for i in range(2)])
     begin(1)
-    pl.loop(2, 5)(lambda i: forward(5 * c + i))
+    forward([5 * c + i for i in range(2, 5)])
     send_att(1, c)
 
     dest_f = dest.astype(F32)
@@ -305,6 +307,9 @@
             for j, ref, k in ((0, w0.at[x, ys], ys), (1, w1.at[y, xs], xs)):
                 piece = ref.at[pl.ds(*rows)]
                 rcopy(piece, piece, a1_ssem.at[j, s, q], a1_rsem.at[j, k, q], sibling).wait_recv()
+                if (s, q) in ((3, 0), (1, 1)):
+                    to = dev(x, (y - s + 4) % NY, z, c) if j == 0 else dev((x - s + 4) % NX, y, z, c)
+                    rcopy(piece, piece, a1_ssem.at[j, 2, q], a1_rsem.at[j, k, q], to).start()
                 pass_on(j, k, q)
 
     relay(0)
@@ -486,29 +491,35 @@
             g_v[k] = out[:, SPAD * k : SPAD * (k + 1)].T[:OWN].astype(BF16)
 
     live = ids_col >= 0.0
-
-    def backward(p, gp):
-        at = pl.ds(pl.multiple_of(p * 128, 128), 128)
-        qp, kp, vp = q_v[:, at], k_v[:, at], v_v[:, at]
-        prob = probs[p]
-        pg = dot_nt(both_heads(gp), vp)
-        delta = jnp.sum(prob * pg, axis=1, keepdims=True)
-        sg = (prob * (pg - delta)).astype(BF16)
-        pb = prob.astype(BF16)
-        dq = dot_nn(sg, kp)
-
-        def put(ref, one, two, scale):
-            value = jnp.where(first_head, one, two) * scale
-            ref[:, at] = jnp.where(live, value, 0.0).astype(BF16)
-
-        put(dq_v, dq[:OWN], dq[OWN:], SCALE)
-        put(dk_v, dot_tn(sg[:OWN], qp), dot_tn(sg[OWN:], qp), SCALE)
-        put(dv_v, dot_tn(pb[:OWN], gp), dot_tn(pb[OWN:], gp), 1.0)
+    halves = (slice(0, OWN), slice(OWN, 2 * OWN))
+
+    def backward(part, places):
+        pairs = [5 * part + i for i in places]
+        at = [pl.ds(pl.multiple_of(p * 128, 128), 128) for p in pairs]
+        grads = [g_v[i] for i in places]
+        prob = [probs[p] for p in pairs]
+        pgs = [dot_nt(both_heads(g), v_v[:, a]) for g, a in zip(grads, at)]
+        deltas = [jnp.sum(t * pg, axis=1, keepdims=True) for t, pg in zip(prob, pgs)]
+        sgs = [(t * (pg - d)).astype(BF16) for t, pg, d in zip(prob, pgs, deltas)]
+        pbs = [t.astype(BF16) for t in prob]
+        dqs = [dot_nn(sg, k_v[:, a]) for sg, a in zip(sgs, at)]
+        dks = [[dot_tn(sg[r], q_v[:, a]) for r in halves] for sg, a in zip(sgs, at)]
+        dvs = [[dot_tn(pb[r], g) for r in halves] for pb, g in zip(pbs, grads)]
+
+        def put(ref, a, parts, scale):
+            value = jnp.where(first_head, parts[0], parts[1]) * scale
+            ref[:, a] = jnp.where(live, value, 0.0).astype(BF16)
+
+        for a, dq, dk, dv in zip(at, dqs, dks, dvs):
+            put(dq_v, a, (dq[:OWN], dq[OWN:]), SCALE)
+            put(dk_v, a, dk, SCALE)
+            put(dv_v, a, dv, 1.0)
 
     take_grad(0)
-    pl.loop(0, 5)(lambda i: backward(5 * c + i, g_v[i]))
+    backward(c, (0, 1))
+    backward(c, (2, 3, 4))
     take_grad(1)
-    pl.loop(0, 2)(lambda i: backward(5 * o + i, g_v[i]))
+    backward(o, (0, 1))
     def piece_of(i, q):
         return fall.at[i, pl.ds(*SPREAD[q])]
 
@@ -546,7 +557,7 @@
                         ).start()
             to_sibling(x, q)
 
-    pl.loop(2, 5)(lambda i: backward(5 * o + i, g_v[i]))
+    backward(o, (2, 3, 4))
     outs = [
         pltpu.make_async_copy(src, dst, out_sem.at[i])
         for i, (src, dst) in enumerate(((dq_v, dq_hbm), (dk_v, dk_hbm), (dv_v, dv_hbm)))
@@ -655,19 +666,25 @@
 
 
 def finish(dq_in, dk_in, dv_in, wg_in, dq_out, dk_out, dv_out, wg_out, grads, wg_b, wg_f, sems):
-    pairs = ((dq_in, dq_out), (dk_in, dk_out), (dv_in, dv_out))
-    reads = [pltpu.make_async_copy(pairs[i][0], grads.at[i], sems.at[i]) for i in range(3)]
-    reads.append(pltpu.make_async_copy(wg_in, wg_b, sems.at[3]))
-    writes = [pltpu.make_async_copy(grads.at[i], pairs[i][1], sems.at[i]) for i in range(3)]
-    writes.append(pltpu.make_async_copy(wg_f, wg_out, sems.at[3]))
+    whole = ((dq_in, dq_out), (dk_in, dk_out), (dv_in, dv_out))
+    reads, writes = [], []
+    for q, (top, count) in enumerate(SPREAD):
+        rows = pl.ds(top, count)
+        reads.append(pltpu.make_async_copy(wg_in.at[rows], wg_b.at[rows], sems.at[3, q]))
+        writes.append(pltpu.make_async_copy(wg_f.at[rows], wg_out.at[rows], sems.at[3, q]))
+    for q in range(2):
+        rows = pl.ds(q * (OWN // 2), OWN // 2)
+        for i, (src, dst) in enumerate(whole):
+            held = grads.at[i, rows]
+            reads.append(pltpu.make_async_copy(src.at[rows], held, sems.at[i, q]))
+            writes.append(pltpu.make_async_copy(held, dst.at[rows], sems.at[i, q]))
     for read in reads:
         read.start()
-    for i in range(3):
-        reads[i].wait()
-        writes[i].start()
-    reads[3].wait()
-    wg_f[...] = wg_b[...].astype(F32)
-    for write in writes[3:]:
+    for n, (read, write) in enumerate(zip(reads, writes)):
+        read.wait()
+        if n < 2:
+            top, count = SPREAD[n]
+            wg_f[top : top + count] = wg_b[top : top + count].astype(F32)
         write.start()
     for write in writes:
         write.wait()
@@ -733,7 +750,7 @@
         out_shape=(slots, slots, slots, jax.ShapeDtypeStruct((ROWS, D), F32)),
         in_specs=[any_space] * 4,
         out_specs=(any_space,) * 4,
-        scratch_shapes=[vmem((3, OWN, PAIRS * 128), BF16), vmem((ROWS, D), BF16), vmem((ROWS, D), F32), dma((4,))],
+        scratch_shapes=[vmem((3, OWN, PAIRS * 128), BF16), vmem((ROWS, D), BF16), vmem((ROWS, D), F32), dma((4, 2))],
     )(*grads, weight_grad)
 
 

time: 91.9 us -> 91.3 us (level)
  no operation moved by 1% of the time
where the time goes in v5:
time: 91.3 us; the launch traced here: 91 us
  Pallas kernels  90.2 us (99%)
    pallas_call x1, Pallas kernels, per_device(): pl.pallas_call(kernel, out_shape=(slots, slots, slots, jax.ShapeDtypeStru...  87.8 us
    pallas_call x1, Pallas kernels, per_device(): pl.pallas_call(finish, out_shape=(slots, slots, slots, jax.ShapeDtypeStru...  2.41 us

profile of v5, /device:TPU:1, one launch (start us, length us, event | category | flops | bytes accessed | tf_op | source)
XLA Modules:
  0.0 91.0 jit_solution(9065078709527278483)
XLA Ops:
  0.6 87.8 %shard_map.102 = (bf16[192,1280]{1,0:T(8,128)(2,1)}, bf16[192,1280]{1,0:T(8,128)(2,1)}, bf16[192,1280]{1,0:T(8,128)(2,1)}, bf16[80,2560]{1,0:T(8,128)(2,1)}) custom-call(bf16[128,2560]{1,0:T(8,128)(2,1)} %cot_hbm.1, bf16[80,2560]{1,0:T(8,128)(2,1)} %w_hbm.1, bf16[192,1280]{1,0:T(8,128)(2,1)} %q_hbm.1, bf16[192,1280]{1,0:T(8,128)(2,1)} %k_hbm.1, ...), custom_call_target="tpu_custom_call" | custom-call | tf_op jit(solution)/shard_map/pallas_call | solution.py:699
  88.4 2.4 %shard_map.103 = (bf16[192,1280]{1,0:T(8,128)(2,1)}, bf16[192,1280]{1,0:T(8,128)(2,1)}, bf16[192,1280]{1,0:T(8,128)(2,1)}, f32[80,2560]{1,0:T(8,128)}) custom-call(bf16[192,1280]{1,0:T(8,128)(2,1)} %get-tuple-element.8.dq_in, bf16[192,1280]{1,0:T(8,128)(2,1)} %get-tuple-element.9.dk_in, bf16[192,1280]{1,0:T(8,128)(2,1)} %get-tuple-element.10.dv_in, ...), custom_call_target="tpu_custom_call" | custom-call | tf_op jit(solution)/shard_map/pallas_call | solution.py:748
